TPU v7x, 32 devices: a whole 2x2x4 slice. The times are simulated.
32 devices in a mesh: sec: 16 (over z, x, core), blk: 2 (over y).
Axes of the slice: x: 2, y: 2, z: 4, core: 2. Of those that a mesh axis runs over, the one named last changes fastest.
Arguments:
- corner: bfloat16 [2048, 256], P('sec'), may hold values from -0.375 to 0.375
- edge_tiles: bfloat16 [2048, 16, 256], P(('sec', 'blk')), may hold values from -6 to 6
- projector: bfloat16 [2048, 16, 256], P(('sec', 'blk')), may hold values from -0.09375 to 0.09375
- sector_of: int32 [2048], P(('sec', 'blk')), may hold values from 0 to 7
Outputs:
- new_corner: float32 [2048, 256], P(('sec', 'blk'))
All inputs are finite; a program needn't handle non-finite values.
Results may differ from a plain program's by a relative error of at most 0.0003.
Values may be sent and summed in bfloat16 or wider, within the bound.
No kernel may reach another device: no remote copies, remote signals or barrier semaphores. Data moves between devices by JAX's collectives and lax.ppermute only.
A program may use at most 64 MiB of HBM per device.

v0:
```python
import jax
import jax.numpy as jnp
from jax import lax
from jax.sharding import PartitionSpec as P


def fold_tiles(first_op, second_op, sectors, sector_count):
    width = first_op.shape[2]
    labels = jnp.arange(sector_count, dtype=jnp.int32)

    def advance(running, group_item):
        proj_group, other_group, sector_group = group_item
        contrib = jnp.einsum(
            "trs,tru->tsu",
            proj_group.astype(jnp.float32),
            other_group,
            precision=lax.Precision.HIGHEST,
        )
        indicator = (sector_group[:, None] == labels[None, :]).astype(jnp.float32)
        return (
            running
            + jnp.einsum("tb,tsu->bsu", indicator, contrib, precision=lax.Precision.HIGHEST),
            None,
        )

    items = (
        first_op.reshape(-1, 8, first_op.shape[1], width),
        second_op.reshape(-1, 8, second_op.shape[1], second_op.shape[2]),
        sectors.reshape(-1, 8),
    )
    summed, _ = lax.scan(
        advance, jnp.zeros((sector_count, width, second_op.shape[2]), jnp.float32), items
    )
    return summed


def local(corner, edge_tiles, projector, sector_of):
    sec_count = lax.axis_size("sec")
    tile_count, tile_rows, width = edge_tiles.shape
    per_peer = tile_count // sec_count
    corner_all = lax.all_gather(corner, "sec", axis=0, tiled=True)
    sector_count = corner_all.shape[0] // width
    blocks3 = corner_all.reshape(sector_count, width, width)

    def image_of(group_item):
        tile_group, sector_group = group_item
        chosen = jnp.take(blocks3, sector_group, axis=0)
        return jnp.einsum("trs,tsu->tru", tile_group, chosen, preferred_element_type=jnp.float32)

    images = lax.map(
        image_of, (edge_tiles.reshape(-1, 8, tile_rows, width), sector_of.reshape(-1, 8))
    )
    arrived, arrived_sec = (
        lax.all_to_all(
            images.reshape(sec_count, per_peer, tile_rows, width),
            "sec",
            split_axis=0,
            concat_axis=0,
            tiled=True,
        ),
        lax.all_to_all(
            sector_of.reshape(sec_count, per_peer), "sec", split_axis=0, concat_axis=0, tiled=True
        ),
    )
    summed = fold_tiles(
        projector,
        arrived.reshape(tile_count, tile_rows, width),
        arrived_sec.reshape(tile_count),
        sector_count,
    )
    flat_sum = summed.reshape(sector_count * width, width)
    group_rows = lax.psum_scatter(flat_sum, "sec", scatter_dimension=0, tiled=True)
    my_rows = lax.psum_scatter(group_rows, "blk", scatter_dimension=0, tiled=True)
    return my_rows


def solution(mesh):
    in_specs = (
        P("sec", None),
        P(("sec", "blk"), None, None),
        P(("sec", "blk"), None, None),
        P(("sec", "blk")),
    )
    out_specs = P(("sec", "blk"), None)
    return jax.shard_map(local, mesh=mesh, in_specs=in_specs, out_specs=out_specs, check_vma=False)
```

profile of v0, /device:TPU:0, one launch (start us, length us, event | category | flops | bytes accessed | tf_op | source)
XLA Modules:
  0.0 228.0 jit_solution(10447487529479367115)
XLA Ops:
  6.5 0.7 all-gather.2.cloned.1.call-update
  7.3 1.3 all_to_all.9
  8.6 7.4 %all-to-all-start = ((s32[16,1,4]{2,1,0:T(1,128)}), s32[16,1,4]{2,1,0:T(1,128)S(1)}, u32[]{:S(2)}, u32[]{:S(2)}) async-start(s32[16,1,4]{2,1,0:T(1,128)} %bitcast.5), calls=%async_computation | async-start | bytes 16384 | tf_op jit(solution)/shard_map/all_to_all | solution.py:61
  16.0 0.7 reshape.62
  16.7 33.5 %all-gather.2.cloned.1.call-done = bf16[2048,256]{1,0:T(8,128)(2,1)} async-done(((bf16[128,256]{1,0:T(8,128)(2,1)}), bf16[2048,256]{1,0:T(8,128)(2,1)}) %all-gather.2.cloned.1.call-update) | async-done | bytes 1048592 | tf_op jit(solution)/shard_map/all_gather | solution.py:41
  50.2 29.7 %while.21 = (s32[]{:T(128)}, f32[8,8,16,256]{3,2,1,0:T(8,128)}, bf16[8,8,16,256]{3,2,1,0:T(8,128)(2,1)}, s32[8,8]{1,0:T(8,128)S(1)}, bf16[8,256,256]{2,1,0:T(8,128)(2,1)}, /*index=5*/s32[]{:T(128)}) while((s32[]{:T(128)}, f32[8,8,16,256]{3,2,1,0:T(8,128)}, bf16[8,8,16,256]{3,2,1,0:T(8,128)(2,1)}, s32[8,8]{1,0:T(8,128)S(1)}, ...), condition=%wide.region_1.2_spmd, body=%wide.region_0.1_spmd.sunk | while | flops 17302600 | bytes 3347717 | solution.py:50
  50.2 1.8 gather_fusion
  52.1 1.8 fusion.38
  53.9 1.8 gather_fusion
  55.8 1.8 fusion.38
  57.6 1.8 gather_fusion
  59.5 1.8 fusion.38
  61.3 1.8 gather_fusion
  63.2 1.8 fusion.38
  65.0 1.8 gather_fusion
  66.9 1.8 fusion.38
  68.8 1.8 gather_fusion
  70.6 1.8 fusion.38
  72.4 1.8 gather_fusion
  74.3 1.8 fusion.38
  76.2 1.8 gather_fusion
  78.0 1.8 fusion.38
  79.9 3.7 %all-to-all-start.1 = ((f32[16,4,16,256]{3,2,1,0:T(8,128)}), f32[16,4,16,256]{3,2,1,0:T(8,128)S(1)}, u32[]{:S(2)}, u32[]{:S(2)}) async-start(f32[16,4,16,256]{3,2,1,0:T(8,128)} %bitcast.9), calls=%async_computation.1 | async-start | bytes 2097152 | tf_op jit(solution)/shard_map/all_to_all | solution.py:54
  83.5 0.0 reduce-scatter.3.cloned.1.call-start
  83.6 0.6 broadcast.46
  84.2 0.7 reduce.3
  84.9 0.1 reshape_reshape.6
  85.0 21.5 %all-to-all-done.1 = f32[16,4,16,256]{3,2,1,0:T(8,128)S(1)} async-done(((f32[16,4,16,256]{3,2,1,0:T(8,128)}), f32[16,4,16,256]{3,2,1,0:T(8,128)S(1)}, u32[]{:S(2)}, u32[]{:S(2)}) %all-to-all-start.1) | async-done | bytes 1048608 | tf_op jit(solution)/shard_map/all_to_all | solution.py:54
  106.4 37.5 %while.22 = (s32[]{:T(128)}, f32[8,256,256]{2,0,1:T(8,128)S(1)}, s32[8,8]{1,0:T(8,128)S(1)}, bf16[8,8,16,256]{3,2,1,0:T(8,128)(2,1)}, f32[8,8,16,256]{3,2,1,0:T(8,128)S(1)}, /*index=5*/s32[]{:T(128)}, s32[]{:T(128)}) while((s32[]{:T(128)}, f32[8,256,256]{2,0,1:T(8,128)S(1)}, s32[8,8]{1,0:T(8,128)S(1)}, ...), condition=%wide.region_3.4_spmd.clone, body=%wide.region_2.3_spmd.clone.sunk | while | flops 152043584 | bytes 8586435 | solution.py:31
  106.4 1.9 fusion.43
  108.3 2.8 %select_add_fusion.2 = f32[8,256,256]{2,0,1:T(8,128)S(1)} fusion(f32[8,256,256]{2,0,1:T(8,128)S(1)} %get-tuple-element.194, f32[8,256,256]{2,1,0:T(8,128)S(1)} %fusion.43, pred[]{:T(512)S(6)} %compare.3, s32[8]{0:T(128)S(1)} %fusion.44), kind=kOutput, calls=%fused_computation.19.clone.1 | convolution fusion | flops 51380288 | bytes 6291489 | tf_op jit(solution)/shard_map/while/body/eval_jaxpr/tb,tsu->bsu/dot_general | solution.py:22
  111.1 1.9 fusion.43
  113.0 2.8 %select_add_fusion.2 = f32[8,256,256]{2,0,1:T(8,128)S(1)} fusion(f32[8,256,256]{2,0,1:T(8,128)S(1)} %get-tuple-element.194, f32[8,256,256]{2,1,0:T(8,128)S(1)} %fusion.43, pred[]{:T(512)S(6)} %compare.3, s32[8]{0:T(128)S(1)} %fusion.44), kind=kOutput, calls=%fused_computation.19.clone.1 | convolution fusion | flops 51380288 | bytes 6291489 | tf_op jit(solution)/shard_map/while/body/eval_jaxpr/tb,tsu->bsu/dot_general | solution.py:22
  115.8 1.9 fusion.43
  117.7 2.8 %select_add_fusion.2 = f32[8,256,256]{2,0,1:T(8,128)S(1)} fusion(f32[8,256,256]{2,0,1:T(8,128)S(1)} %get-tuple-element.194, f32[8,256,256]{2,1,0:T(8,128)S(1)} %fusion.43, pred[]{:T(512)S(6)} %compare.3, s32[8]{0:T(128)S(1)} %fusion.44), kind=kOutput, calls=%fused_computation.19.clone.1 | convolution fusion | flops 51380288 | bytes 6291489 | tf_op jit(solution)/shard_map/while/body/eval_jaxpr/tb,tsu->bsu/dot_general | solution.py:22
  120.5 1.9 fusion.43
  122.4 2.8 %select_add_fusion.2 = f32[8,256,256]{2,0,1:T(8,128)S(1)} fusion(f32[8,256,256]{2,0,1:T(8,128)S(1)} %get-tuple-element.194, f32[8,256,256]{2,1,0:T(8,128)S(1)} %fusion.43, pred[]{:T(512)S(6)} %compare.3, s32[8]{0:T(128)S(1)} %fusion.44), kind=kOutput, calls=%fused_computation.19.clone.1 | convolution fusion | flops 51380288 | bytes 6291489 | tf_op jit(solution)/shard_map/while/body/eval_jaxpr/tb,tsu->bsu/dot_general | solution.py:22
  125.2 1.9 fusion.43
  127.1 2.8 %select_add_fusion.2 = f32[8,256,256]{2,0,1:T(8,128)S(1)} fusion(f32[8,256,256]{2,0,1:T(8,128)S(1)} %get-tuple-element.194, f32[8,256,256]{2,1,0:T(8,128)S(1)} %fusion.43, pred[]{:T(512)S(6)} %compare.3, s32[8]{0:T(128)S(1)} %fusion.44), kind=kOutput, calls=%fused_computation.19.clone.1 | convolution fusion | flops 51380288 | bytes 6291489 | tf_op jit(solution)/shard_map/while/body/eval_jaxpr/tb,tsu->bsu/dot_general | solution.py:22
  129.9 1.9 fusion.43
  131.8 2.8 %select_add_fusion.2 = f32[8,256,256]{2,0,1:T(8,128)S(1)} fusion(f32[8,256,256]{2,0,1:T(8,128)S(1)} %get-tuple-element.194, f32[8,256,256]{2,1,0:T(8,128)S(1)} %fusion.43, pred[]{:T(512)S(6)} %compare.3, s32[8]{0:T(128)S(1)} %fusion.44), kind=kOutput, calls=%fused_computation.19.clone.1 | convolution fusion | flops 51380288 | bytes 6291489 | tf_op jit(solution)/shard_map/while/body/eval_jaxpr/tb,tsu->bsu/dot_general | solution.py:22
  134.6 1.9 fusion.43
  136.5 2.8 %select_add_fusion.2 = f32[8,256,256]{2,0,1:T(8,128)S(1)} fusion(f32[8,256,256]{2,0,1:T(8,128)S(1)} %get-tuple-element.194, f32[8,256,256]{2,1,0:T(8,128)S(1)} %fusion.43, pred[]{:T(512)S(6)} %compare.3, s32[8]{0:T(128)S(1)} %fusion.44), kind=kOutput, calls=%fused_computation.19.clone.1 | convolution fusion | flops 51380288 | bytes 6291489 | tf_op jit(solution)/shard_map/while/body/eval_jaxpr/tb,tsu->bsu/dot_general | solution.py:22
  139.3 1.9 fusion.43
  141.2 2.8 %select_add_fusion.2 = f32[8,256,256]{2,0,1:T(8,128)S(1)} fusion(f32[8,256,256]{2,0,1:T(8,128)S(1)} %get-tuple-element.194, f32[8,256,256]{2,1,0:T(8,128)S(1)} %fusion.43, pred[]{:T(512)S(6)} %compare.3, s32[8]{0:T(128)S(1)} %fusion.44), kind=kOutput, calls=%fused_computation.19.clone.1 | convolution fusion | flops 51380288 | bytes 6291489 | tf_op jit(solution)/shard_map/while/body/eval_jaxpr/tb,tsu->bsu/dot_general | solution.py:22
  144.0 2.0 copy.9
  146.1 63.8 %reduce-scatter.3.cloned.1.call-done = f32[128,256]{1,0:T(8,128)} async-done(((f32[2048,256]{1,0:T(8,128)}), f32[128,256]{1,0:T(8,128)}) %reduce-scatter.3.cloned.1.call-update) | async-done | bytes 131088 | tf_op jit(solution)/shard_map/reduce_scatter | solution.py:72
  209.9 11.6 %reduce-scatter.5.cloned.1.call-done = f32[64,256]{1,0:T(8,128)} async-done(((f32[128,256]{1,0:T(8,128)}), f32[64,256]{1,0:T(8,128)}) %reduce-scatter.5.cloned.1.call-update) | async-done | bytes 65552 | tf_op jit(solution)/shard_map/reduce_scatter | solution.py:73
  (39 shorter events, 0.3 us)
Async XLA Ops:
  6.5 43.7 %all-gather.2.cloned.1.call-start = ((), (), s32[]{:S(2)}) async-start(), calls=%async_computation.4 | async-start | bytes 1114112 | tf_op jit(solution)/shard_map/all_gather | solution.py:41
  8.6 71.3 %all-to-all-start = ((s32[16,1,4]{2,1,0:T(1,128)}), s32[16,1,4]{2,1,0:T(1,128)S(1)}, u32[]{:S(2)}, u32[]{:S(2)}) async-start(s32[16,1,4]{2,1,0:T(1,128)} %bitcast.5), calls=%async_computation | async-start | bytes 16384 | tf_op jit(solution)/shard_map/all_to_all | solution.py:61
  79.9 26.6 %all-to-all-start.1 = ((f32[16,4,16,256]{3,2,1,0:T(8,128)}), f32[16,4,16,256]{3,2,1,0:T(8,128)S(1)}, u32[]{:S(2)}, u32[]{:S(2)}) async-start(f32[16,4,16,256]{3,2,1,0:T(8,128)} %bitcast.9), calls=%async_computation.1 | async-start | bytes 2097152 | tf_op jit(solution)/shard_map/all_to_all | solution.py:54
  83.5 126.4 %reduce-scatter.3.cloned.1.call-start = ((), (), s32[]{:S(2)}) async-start(), calls=%async_computation.5 | async-start | bytes 2228224 | tf_op jit(solution)/shard_map/reduce_scatter | solution.py:72
  146.0 75.5 %reduce-scatter.5.cloned.1.call-start = ((), (), s32[]{:S(2)}) async-start(), calls=%async_computation.6 | async-start | bytes 196608 | tf_op jit(solution)/shard_map/reduce_scatter | solution.py:73
Sparse Core Ops, SparseCore 0:
  9.5 40.6 all-gather.1
  146.1 63.7 reduce-scatter.2
  212.2 9.2 reduce-scatter.4
where the time goes:
time: 229 us; the launch traced here: 228 us
  waiting for transfers between devices  131 us (57%)
  matrix products  51.8 us (23%)
  local copies, waits for them, and re-layouts  19.5 us (9%)
  between operations  13.1 us (6%)
  starting transfers between devices  11.1 us (5%)
    reduce_scatter x1, waiting for transfers between devices, local(): lax.psum_scatter(flat_sum, 'sec', scatter_dimension=0, tiled=True)  63.8 us
    all_gather x1, waiting for transfers between devices, local(): corner_all = lax.all_gather(corner, 'sec', axis=0, tiled=True)  33.5 us
    dot_general x8, matrix products, advance(): jnp.einsum('tb,tsu->bsu', indicator, contrib, precision=lax.Precision.HIG...  22.2 us
    all_to_all x1, waiting for transfers between devices, local(): lax.all_to_all(images.reshape(sec_count, per_peer, tile_rows, width), 'se...  21.5 us
    dot_general x8, matrix products, advance(): jnp.einsum('trs,tru->tsu', proj_group.astype(jnp.float32), other_group, p...  15 us
    gather x8, local copies, waits for them, and re-layouts, image_of(): chosen = jnp.take(blocks3, sector_group, axis=0)  14.7 us
    dot_general x8, matrix products, image_of(): jnp.einsum('trs,tsu->tru', tile_group, chosen, preferred_element_type=jnp...  14.6 us
    reduce_scatter x1, waiting for transfers between devices, local(): lax.psum_scatter(group_rows, 'blk', scatter_dimension=0, tiled=True)  11.6 us
  transfers between devices with their start and end apart: 5, of which 4 were waited for; matrix products, arithmetic and copies ran while one was open for 14% of the time, Pallas kernels for 0%

commit v1 on v0

v1 whole, which is shorter than its diff:
```python
import functools

import jax
import jax.numpy as jnp
from jax import lax
from jax.experimental import pallas as pl
from jax.experimental.pallas import tpu as pltpu
from jax.sharding import PartitionSpec as P

VMEM_LIMIT = 48 * 1024 * 1024


def transpose_kernel(p_ref, o_ref):
    groups, rows, _ = p_ref.shape
    for g in range(groups):
        o_ref[g] = p_ref[g].T


def transpose_rows(p3):
    groups, rows, width = p3.shape
    if rows % 128 or width % 128:
        return jnp.swapaxes(p3, 1, 2)
    return pl.pallas_call(
        transpose_kernel,
        out_shape=jax.ShapeDtypeStruct((groups, width, rows), p3.dtype),
        compiler_params=pltpu.CompilerParams(vmem_limit_bytes=VMEM_LIMIT),
    )(p3)


def fold_kernel(sector_count, lane_ref, slab_ref, *refs):
    edge_refs, out_ref = refs[:-1], refs[-1]
    peers, _, depth = lane_ref.shape
    blk_count = slab_ref.shape[1]
    step = edge_refs[0].shape[1]
    for d in range(peers):
        left = jnp.concatenate([slab_ref[d, j] for j in range(blk_count)], axis=1)
        lane = lane_ref[d]
        rows = []
        for b in range(sector_count):
            chosen = (lane == b).astype(jnp.float32).astype(left.dtype)
            rows.append(left * chosen)
        right = jnp.concatenate([e[d] for e in edge_refs], axis=0)
        part = jnp.dot(
            jnp.concatenate(rows, axis=0), right, preferred_element_type=jnp.float32
        ).reshape(out_ref.shape)
        if d == 0:
            out_ref[...] = part
        else:
            out_ref[...] += part


def fold_tiles(slabs, edges, lanes, sector_count):
    peers, blk_count, cols, depth = slabs.shape
    width = edges[0].shape[2]
    if depth % 128 or cols % 16 or edges[0].shape[1] % 16:
        left = jnp.moveaxis(slabs, 2, 1).reshape(peers, 1, cols, blk_count * depth)
        labels = jnp.arange(sector_count, dtype=jnp.int32)[None, :, None, None]
        left = left * (lanes[:, :, None, :] == labels).astype(left.dtype)
        right = jnp.concatenate(edges, axis=1)
        return jnp.einsum("dbsk,dku->bsu", left, right, preferred_element_type=jnp.float32)
    return pl.pallas_call(
        functools.partial(fold_kernel, sector_count),
        out_shape=jax.ShapeDtypeStruct((sector_count, cols, width), jnp.float32),
        compiler_params=pltpu.CompilerParams(vmem_limit_bytes=VMEM_LIMIT),
    )(lanes, slabs, *edges)


def pairwise(first, second, odd):
    return jnp.where(odd, second, first), jnp.where(odd, first, second)


def local(corner, edge_tiles, projector, sector_of):
    sec_count, blk_count = lax.axis_size("sec"), lax.axis_size("blk")
    me, my_blk = lax.axis_index("sec"), lax.axis_index("blk")
    tile_count, tile_rows, width = edge_tiles.shape
    columns = sec_count // 2
    per_peer = tile_count // sec_count
    slab_depth = per_peer * tile_rows
    corner_rows = corner.shape[0]
    sector_count = corner_rows * sec_count // width
    out_rows = corner_rows // blk_count
    spread = columns // sector_count
    sibling = [(i, i ^ 1) for i in range(sec_count)]

    def turn(array, by):
        return lax.ppermute(array, "blk", [(j, (j + by) % blk_count) for j in range(blk_count)])

    edges3 = edge_tiles.reshape(sec_count, slab_depth, width)
    edge_turns = [edges3] + [turn(edges3, k) for k in range(1, blk_count)]
    sector_turns = [sector_of] + [turn(sector_of, k) for k in range(1, blk_count)]
    edge_pairs = [(e, lax.ppermute(e, "sec", sibling)) for e in edge_turns]
    sector_all = jnp.stack(sector_turns)
    sector_both = jnp.stack([sector_all, lax.ppermute(sector_all, "sec", sibling)])

    slabs = transpose_rows(projector.reshape(columns, 2 * slab_depth, width))
    slabs = slabs.reshape(columns, spread, 2, blk_count, out_rows, 2 * slab_depth)
    slabs = jnp.moveaxis(slabs, 1, 3)
    slabs = slabs.reshape(sec_count * blk_count, spread * out_rows, 2 * slab_depth)
    arrived = lax.all_to_all(slabs, ("sec", "blk"), split_axis=0, concat_axis=0, tiled=True)
    arrived = arrived.reshape(sec_count, blk_count, spread * out_rows, 2 * slab_depth)

    odd = me % 2 == 1
    turned = (my_blk - jnp.arange(blk_count)) % blk_count
    edges = []
    for j in range(blk_count):
        own, other = edge_pairs[0]
        for k in range(1, blk_count):
            own = jnp.where((my_blk - k) % blk_count == j, edge_pairs[k][0], own)
            other = jnp.where((my_blk - k) % blk_count == j, edge_pairs[k][1], other)
        edges.extend(pairwise(own, other, odd))
    sector_both = jnp.where(odd, sector_both[::-1], sector_both)
    sector_both = jnp.take(sector_both, turned, axis=1)
    lanes = jnp.moveaxis(sector_both.reshape(2, blk_count, sec_count, per_peer), 2, 0)
    lanes = jnp.swapaxes(lanes, 1, 2)
    lanes = jnp.repeat(lanes.reshape(sec_count, 1, -1), tile_rows, axis=2)

    partial = fold_tiles(arrived, edges, lanes, sector_count)
    partial = partial.reshape(columns, out_rows, width)
    groups = [[2 * n + c for n in range(columns)] for c in range(2)]
    received = lax.all_to_all(
        partial, "sec", split_axis=0, concat_axis=0, tiled=True, axis_index_groups=groups
    )
    rows = jnp.sum(received, axis=0)

    share = 2 * spread
    place = me % share
    block = jnp.zeros((share, corner_rows, width), corner.dtype)
    for k in range(share):
        ring = [(i, i // share * share + (i % share + k) % share) for i in range(sec_count)]
        piece = corner if k == 0 else lax.ppermute(corner, "sec", ring)
        block = lax.dynamic_update_index_in_dim(block, piece, (place - k) % share, 0)
    block = block.reshape(width, width)
    high = lax.reduce_precision(rows, exponent_bits=8, mantissa_bits=7)
    low = (rows - high).astype(jnp.bfloat16)
    both = jnp.dot(
        jnp.concatenate([high.astype(jnp.bfloat16), low], axis=0), block, preferred_element_type=jnp.float32
    )
    return both[:out_rows] + both[out_rows:]


def solution(mesh):
    in_specs = (
        P("sec", None),
        P(("sec", "blk"), None, None),
        P(("sec", "blk"), None, None),
        P(("sec", "blk")),
    )
    out_specs = P(("sec", "blk"), None)
    return jax.shard_map(local, mesh=mesh, in_specs=in_specs, out_specs=out_specs, check_vma=False)
```

time: 229 us -> 49.2 us (0.21)
  waiting for transfers between devices: 131 us -> 24.7 us
  matrix products: 51.8 us -> 0.15 us
  local copies, waits for them, and re-layouts: 19.5 us -> 3.76 us
  between operations: 13.1 us -> 0.23 us
  starting transfers between devices: 11.1 us -> 14.6 us
  Pallas kernels: 0 us -> 3.03 us
    reduce_scatter x2 -> x0, waiting for transfers between devices: 75.4 us -> none  [the longest x1 63.8 us: local(): lax.psum_scatter(flat_sum, 'sec', scatter_dimension=0, tiled=True)]
    dot_general x24 -> x1, matrix products: 51.8 us -> 0.15 us  [local(): jnp.dot(jnp.concatenate([high.astype(jnp.bfloat16), low], axis=0), block,...]
    all_gather x1 -> x0, waiting for transfers between devices: 33.5 us -> none  [local(): corner_all = lax.all_gather(corner, 'sec', axis=0, tiled=True)]
    gather x8 -> x3, local copies, waits for them, and re-layouts: 14.7 us -> 0.66 us  [local(): sector_both = jnp.take(sector_both, turned, axis=1)]
    ppermute x0 -> x6, waiting for transfers between devices: none -> 7.22 us  [the longest x2 5.52 us: turn(): lax.ppermute(array, 'blk', [(j, (j + by) % blk_count) for j in range(blk_...]
    ppermute x0 -> x6, starting transfers between devices: none -> 4.28 us  [the longest x2 3.61 us: turn(): lax.ppermute(array, 'blk', [(j, (j + by) % blk_count) for j in range(blk_...]
    all_to_all x2, waiting for transfers between devices: 21.5 us -> 17.5 us  [the longest x1 13.6 us: local(): lax.all_to_all(partial, 'sec', split_axis=0, concat_axis=0, tiled=True, a...]
    pallas_call x0 -> x2, Pallas kernels: none -> 3.03 us  [the longest x1 2.04 us: fold_tiles(): pl.pallas_call(functools.partial(fold_kernel, sector_count), out_shape=ja...]
  transfers between devices with their start and end apart: 5 -> 8, of which waited for: 4 -> 5; matrix products, arithmetic and copies ran while one was open for 14% -> 6% of each run, Pallas kernels for 0% -> 2%
where the time goes in v1:
time: 49.2 us; the launch traced here: 48.8 us
  waiting for transfers between devices  24.7 us (50%)
  starting transfers between devices  14.6 us (30%)
  local copies, waits for them, and re-layouts  3.76 us (8%)
  Pallas kernels  3.03 us (6%)
  other arithmetic  2.36 us (5%)
    all_to_all x1, waiting for transfers between devices, local(): lax.all_to_all(partial, 'sec', split_axis=0, concat_axis=0, tiled=True, a...  13.6 us
    all_to_all x1, starting transfers between devices, local(): lax.all_to_all(slabs, ('sec', 'blk'), split_axis=0, concat_axis=0, tiled=...  5.71 us
    ppermute x2, waiting for transfers between devices, turn(): lax.ppermute(array, 'blk', [(j, (j + by) % blk_count) for j in range(blk_...  5.52 us
    all_to_all x1, starting transfers between devices, local(): lax.all_to_all(partial, 'sec', split_axis=0, concat_axis=0, tiled=True, a...  4.58 us
    all_to_all x1, waiting for transfers between devices, local(): lax.all_to_all(slabs, ('sec', 'blk'), split_axis=0, concat_axis=0, tiled=...  3.88 us
    ppermute x2, starting transfers between devices, turn(): lax.ppermute(array, 'blk', [(j, (j + by) % blk_count) for j in range(blk_...  3.61 us
    unnamed x14, local copies, waits for them, and re-layouts  2.65 us
    pallas_call x1, Pallas kernels, fold_tiles(): pl.pallas_call(functools.partial(fold_kernel, sector_count), out_shape=ja...  2.04 us
  transfers between devices with their start and end apart: 8, of which 5 were waited for; matrix products, arithmetic and copies ran while one was open for 6% of the time, Pallas kernels for 2%

profile of v1, /device:TPU:0, one launch (start us, length us, event | category | flops | bytes accessed | tf_op | source)
XLA Modules:
  0.0 48.8 jit_solution(5128137537720118907)
XLA Ops:
  0.0 0.0 copy-start.6
  0.0 3.0 %collective-permute-start.2 = (bf16[16,64,256]{2,1,0:T(8,128)(2,1)}, bf16[16,64,256]{2,1,0:T(8,128)(2,1)S(1)}, u32[]{:S(2)}, u32[]{:S(2)}) collective-permute-start(bf16[16,64,256]{2,1,0:T(8,128)(2,1)} %bitcast.31), channel_id=1, source_target_pairs={{0,1},{1,0},{2,3},{3,2},{4,5},{5,4},{6,7},{7,6},{8,9},{9,8},{10,11... | collective-permute-start | bytes 1572872 | tf_op jit(solution)/shard_map/ppermute | solution.py:86
  3.0 0.0 collective-permute-start.4
  3.0 0.0 copy-done.6
  3.0 0.6 %collective-permute-start = (s32[64]{0:T(128)S(1)}, s32[64]{0:T(128)S(1)}, u32[]{:S(2)}, u32[]{:S(2)}) collective-permute-start(s32[64]{0:T(128)S(1)} %copy-done.6), channel_id=1, source_target_pairs={{0,1},{1,0},{2,3},{3,2},{4,5},{5,4},{6,7},{7,6},{8,9},{9,8},{10,11... | collective-permute-start | bytes 776 | tf_op jit(solution)/shard_map/ppermute | solution.py:86
  3.6 0.0 copy-start
  3.6 1.0 %copy-done = bf16[64,16,256]{2,1,0:T(8,128)(2,1)S(1)} copy-done((bf16[64,16,256]{2,1,0:T(8,128)(2,1)S(1)}, bf16[64,16,256]{2,1,0:T(8,128)(2,1)}, u32[]{:S(2)}) %copy-start) | copy-done | bytes 524312
  4.7 1.0 %shard_map.46 = bf16[8,256,128]{2,1,0:T(8,128)(2,1)} custom-call(bf16[8,128,256]{2,1,0:T(8,128)(2,1)S(1)} %bitcast.30), custom_call_target="tpu_custom_call" | custom-call | tf_op jit(solution)/shard_map/pallas_call | solution.py:23
  5.6 5.7 %all-to-all-start = ((bf16[32,64,128]{2,1,0:T(8,128)(2,1)}), bf16[32,64,128]{2,1,0:T(8,128)(2,1)S(1)}, u32[]{:S(2)}, u32[]{:S(2)}) async-start(bf16[32,64,128]{2,1,0:T(8,128)(2,1)} %bitcast.11), calls=%async_computation | async-start | bytes 1048576 | tf_op jit(solution)/shard_map/all_to_all | solution.py:99
  11.4 0.0 copy-start.1
  11.5 5.5 %collective-permute-done = s32[64]{0:T(128)S(1)} collective-permute-done((s32[64]{0:T(128)S(1)}, s32[64]{0:T(128)S(1)}, u32[]{:S(2)}, u32[]{:S(2)}) %collective-permute-start) | collective-permute-done | bytes 288 | tf_op jit(solution)/shard_map/ppermute | solution.py:86
  17.0 0.0 collective-permute-start.1
  17.0 0.0 collective-permute-done.2
  17.0 0.0 copy-start.2
  17.0 0.5 collective-permute-start.3
  17.5 0.6 %collective-permute-done.1 = s32[2,64]{1,0:T(2,128)S(1)} collective-permute-done((s32[2,64]{1,0:T(2,128)S(1)}, s32[2,64]{1,0:T(2,128)S(1)}, u32[]{:S(2)}, u32[]{:S(2)}) %collective-permute-start.1) | collective-permute-done | bytes 544 | tf_op jit(solution)/shard_map/ppermute | solution.py:93
  18.2 0.6 %gather_fusion = s32[2,2,64]{2,1,0:T(2,128)S(1)} fusion(s32[2,2,64]{2,0,1:T(2,128)S(1)} %broadcast_select_fusion.8, s32[1024]{0:T(1024)S(1)} %pad_clamp_fusion), kind=kCustom, calls=%fused_computation | custom fusion | bytes 2056 | tf_op jit(solution)/shard_map/jit(_take)/gather | solution.py:112
  18.8 0.1 gather.7
  18.8 0.1 select_bitcast_fusion
  18.9 0.1 copy.8
  19.0 0.1 copy.9
  19.1 0.1 broadcast_in_dim.27
  19.2 0.1 broadcast_in_dim.28.lane_ref
  19.3 0.0 collective-permute-done.4
  19.3 0.0 copy-start.3
  19.3 0.0 collective-permute-done.3
  19.4 0.0 copy-done.2
  19.4 0.8 %copy-done.3 = bf16[16,64,256]{2,1,0:T(8,128)(2,1)} copy-done((bf16[16,64,256]{2,1,0:T(8,128)(2,1)}, bf16[16,64,256]{2,1,0:T(8,128)(2,1)S(1)}, u32[]{:S(2)}) %copy-start.3) | copy-done | bytes 524312
  20.2 0.0 copy-start.4
  20.2 0.8 %copy-done.4 = bf16[16,64,256]{2,1,0:T(8,128)(2,1)} copy-done((bf16[16,64,256]{2,1,0:T(8,128)(2,1)}, bf16[16,64,256]{2,1,0:T(8,128)(2,1)S(1)}, u32[]{:S(2)}) %copy-start.4) | copy-done | bytes 524312
  21.0 0.0 copy-done.1
  21.0 1.5 %broadcast_select_fusion.4 = (bf16[16,64,256]{2,1,0:T(8,128)(2,1)S(1)}, bf16[16,64,256]{2,1,0:T(8,128)(2,1)S(1)}, bf16[16,64,256]{2,1,0:T(8,128)(2,1)S(1)}, bf16[16,64,256]{2,1,0:T(8,128)(2,1)S(1)}) fusion(pred[]{:T(512)S(6)} %eq.22, bf16[16,64,256]{2,1,0:T(8,128)(2,1)} %copy-done.4, bf16[16,64,256]{2,1,0:T(8,128)(2,1)} %copy-done.3, pred[]{:T(512)S(6)} %eq.24, ...), kind=kLoop, calls=%fused_computation.5 | loop fusion | flops 2097152 | bytes 4194307 | tf_op jit(solution)/shard_map/jit(_where)/select_n | solution.py:69
  22.5 3.9 %all-to-all-done = bf16[32,64,128]{2,1,0:T(8,128)(2,1)S(1)} async-done(((bf16[32,64,128]{2,1,0:T(8,128)(2,1)}), bf16[32,64,128]{2,1,0:T(8,128)(2,1)S(1)}, u32[]{:S(2)}, u32[]{:S(2)}) %all-to-all-start) | async-done | bytes 524320 | tf_op jit(solution)/shard_map/all_to_all | solution.py:99
  26.4 2.0 %shard_map.47 = f32[8,64,256]{2,1,0:T(8,128)} custom-call(s32[16,1,256]{2,1,0:T(1,128)S(1)} %broadcast_in_dim.28.lane_ref, bf16[16,2,64,128]{3,2,1,0:T(8,128)(2,1)S(1)} %bitcast.29, bf16[16,64,256]{2,1,0:T(8,128)(2,1)S(1)} %get-tuple-element.8.refs_0_, bf16[16,64,256]{2,1,0:T(8,128)(2,1)S(1)} %get-tuple-element.6.refs_1_, ...), custom_call_target="tpu_custom_call" | custom-call | tf_op jit(solution)/shard_map/pallas_call | solution.py:61
  28.4 0.0 copy-start.5
  28.4 4.6 %all-to-all-start.1 = ((f32[8,64,256]{2,1,0:T(8,128)}), f32[8,64,256]{2,1,0:T(8,128)S(1)}, u32[]{:S(2)}, u32[]{:S(2)}) async-start(f32[8,64,256]{2,1,0:T(8,128)} %shard_map.47), calls=%async_computation.1 | async-start | bytes 1048576 | tf_op jit(solution)/shard_map/all_to_all | solution.py:120
  33.0 0.0 copy-done.5
  33.0 0.2 collective-permute-start.5
  33.2 1.1 %collective-permute-done.5 = bf16[128,256]{1,0:T(8,128)(2,1)S(1)} collective-permute-done((bf16[128,256]{1,0:T(8,128)(2,1)S(1)}, bf16[128,256]{1,0:T(8,128)(2,1)S(1)}, u32[]{:S(2)}, u32[]{:S(2)}) %collective-permute-start.5) | collective-permute-done | bytes 65568 | tf_op jit(solution)/shard_map/ppermute | solution.py:130
  34.3 13.6 %all-to-all-done.1 = f32[8,64,256]{2,1,0:T(8,128)S(1)} async-done(((f32[8,64,256]{2,1,0:T(8,128)}), f32[8,64,256]{2,1,0:T(8,128)S(1)}, u32[]{:S(2)}, u32[]{:S(2)}) %all-to-all-start.1) | async-done | bytes 524320 | tf_op jit(solution)/shard_map/all_to_all | solution.py:120
  48.0 0.2 fusion.1
  48.2 0.6 %slice_add_fusion = f32[64,256]{1,0:T(8,128)} fusion(f32[128,256]{1,0:T(8,128)S(1)} %fusion.1), kind=kLoop, calls=%fused_computation.12 | loop fusion | flops 16384 | bytes 196608 | tf_op jit(solution)/shard_map/add | solution.py:138
  (13 shorter events, 0.2 us)
Async XLA Ops:
  0.0 3.0 %copy-start.6 = (s32[64]{0:T(128)S(1)}, s32[64]{0:T(128)}, u32[]{:S(2)}) copy-start(s32[64]{0:T(128)} %param.7) | copy-start | bytes 772
  0.0 17.0 %collective-permute-start.2 = (bf16[16,64,256]{2,1,0:T(8,128)(2,1)}, bf16[16,64,256]{2,1,0:T(8,128)(2,1)S(1)}, u32[]{:S(2)}, u32[]{:S(2)}) collective-permute-start(bf16[16,64,256]{2,1,0:T(8,128)(2,1)} %bitcast.31), channel_id=1, source_target_pairs={{0,1},{1,0},{2,3},{3,2},{4,5},{5,4},{6,7},{7,6},{8,9},{9,8},{10,11... | collective-permute-start | bytes 1572872 | tf_op jit(solution)/shard_map/ppermute | solution.py:86
  3.0 16.4 %collective-permute-start.4 = (bf16[16,64,256]{2,1,0:T(8,128)(2,1)}, bf16[16,64,256]{2,1,0:T(8,128)(2,1)S(1)}, u32[]{:S(2)}, u32[]{:S(2)}) collective-permute-start(bf16[16,64,256]{2,1,0:T(8,128)(2,1)} %bitcast.32), channel_id=1, source_target_pairs={{0,2},{2,0},{4,6},{6,4},{8,10},{10,8},{12,14},{14,12},{16,18},{18,... | collective-permute-start | bytes 1572872 | tf_op jit(solution)/shard_map/ppermute | solution.py:91
  3.0 14.0 %collective-permute-start = (s32[64]{0:T(128)S(1)}, s32[64]{0:T(128)S(1)}, u32[]{:S(2)}, u32[]{:S(2)}) collective-permute-start(s32[64]{0:T(128)S(1)} %copy-done.6), channel_id=1, source_target_pairs={{0,1},{1,0},{2,3},{3,2},{4,5},{5,4},{6,7},{7,6},{8,9},{9,8},{10,11... | collective-permute-start | bytes 776 | tf_op jit(solution)/shard_map/ppermute | solution.py:86
  3.6 1.0 %copy-start = (bf16[64,16,256]{2,1,0:T(8,128)(2,1)S(1)}, bf16[64,16,256]{2,1,0:T(8,128)(2,1)}, u32[]{:S(2)}) copy-start(bf16[64,16,256]{2,1,0:T(8,128)(2,1)} %param.6) | copy-start | bytes 1572868
  5.6 20.7 %all-to-all-start = ((bf16[32,64,128]{2,1,0:T(8,128)(2,1)}), bf16[32,64,128]{2,1,0:T(8,128)(2,1)S(1)}, u32[]{:S(2)}, u32[]{:S(2)}) async-start(bf16[32,64,128]{2,1,0:T(8,128)(2,1)} %bitcast.11), calls=%async_computation | async-start | bytes 1048576 | tf_op jit(solution)/shard_map/all_to_all | solution.py:99
  11.4 9.6 %copy-start.1 = (bf16[64,16,256]{2,1,0:T(8,128)(2,1)S(1)}, bf16[64,16,256]{2,1,0:T(8,128)(2,1)}, u32[]{:S(2)}) copy-start(bf16[64,16,256]{2,1,0:T(8,128)(2,1)} %param.5) | copy-start | bytes 1572868
  17.0 1.1 %collective-permute-start.1 = (s32[2,64]{1,0:T(2,128)S(1)}, s32[2,64]{1,0:T(2,128)S(1)}, u32[]{:S(2)}, u32[]{:S(2)}) collective-permute-start(s32[2,64]{1,0:T(2,128)S(1)} %pad_add_fusion.1), channel_id=1, source_target_pairs={{0,2},{2,0},{4,6},{6,4},{8,10},{10,8},{12,14},{14,12},{16,18},{18,... | collective-permute-start | bytes 1544 | tf_op jit(solution)/shard_map/ppermute | solution.py:93
  17.0 2.3 %copy-start.2 = (bf16[16,64,256]{2,1,0:T(8,128)(2,1)}, bf16[16,64,256]{2,1,0:T(8,128)(2,1)S(1)}, u32[]{:S(2)}) copy-start(bf16[16,64,256]{2,1,0:T(8,128)(2,1)S(1)} %collective-permute-done.2) | copy-start | bytes 1572868
  17.0 2.3 %collective-permute-start.3 = (bf16[16,64,256]{2,1,0:T(8,128)(2,1)S(1)}, bf16[16,64,256]{2,1,0:T(8,128)(2,1)S(1)}, u32[]{:S(2)}, u32[]{:S(2)}) collective-permute-start(bf16[16,64,256]{2,1,0:T(8,128)(2,1)S(1)} %collective-permute-done.2), channel_id=1, source_target_pairs={{0,2},{2,0},{4,6},{6,4},{8,10},{10,8},{12,14},{14,12},{16,18},{18,... | collective-permute-start | bytes 1572872 | tf_op jit(solution)/shard_map/ppermute | solution.py:91
  19.3 0.8 %copy-start.3 = (bf16[16,64,256]{2,1,0:T(8,128)(2,1)}, bf16[16,64,256]{2,1,0:T(8,128)(2,1)S(1)}, u32[]{:S(2)}) copy-start(bf16[16,64,256]{2,1,0:T(8,128)(2,1)S(1)} %collective-permute-done.4) | copy-start | bytes 1572868
  20.2 0.8 %copy-start.4 = (bf16[16,64,256]{2,1,0:T(8,128)(2,1)}, bf16[16,64,256]{2,1,0:T(8,128)(2,1)S(1)}, u32[]{:S(2)}) copy-start(bf16[16,64,256]{2,1,0:T(8,128)(2,1)S(1)} %collective-permute-done.3) | copy-start | bytes 1572868
  28.4 4.6 %copy-start.5 = (bf16[128,256]{1,0:T(8,128)(2,1)S(1)}, bf16[128,256]{1,0:T(8,128)(2,1)}, u32[]{:S(2)}) copy-start(bf16[128,256]{1,0:T(8,128)(2,1)} %param.4) | copy-start | bytes 196612
  28.4 19.5 %all-to-all-start.1 = ((f32[8,64,256]{2,1,0:T(8,128)}), f32[8,64,256]{2,1,0:T(8,128)S(1)}, u32[]{:S(2)}, u32[]{:S(2)}) async-start(f32[8,64,256]{2,1,0:T(8,128)} %shard_map.47), calls=%async_computation.1 | async-start | bytes 1048576 | tf_op jit(solution)/shard_map/all_to_all | solution.py:120
  33.0 1.3 %collective-permute-start.5 = (bf16[128,256]{1,0:T(8,128)(2,1)S(1)}, bf16[128,256]{1,0:T(8,128)(2,1)S(1)}, u32[]{:S(2)}, u32[]{:S(2)}) collective-permute-start(bf16[128,256]{1,0:T(8,128)(2,1)S(1)} %copy-done.5), channel_id=1, source_target_pairs={{0,2},{2,0},{4,6},{6,4},{8,10},{10,8},{12,14},{14,12},{16,18},{18,... | collective-permute-start | bytes 196616 | tf_op jit(solution)/shard_map/ppermute | solution.py:130

commit v2 on v1

v2 whole, which is shorter than its diff:
```python
import functools

import jax
import jax.numpy as jnp
from jax import lax
from jax.experimental import pallas as pl
from jax.experimental.pallas import tpu as pltpu
from jax.sharding import PartitionSpec as P

VMEM_LIMIT = 48 * 1024 * 1024
TOP = 14
NOTE_ROWS = 8


def slab_kernel(p_hbm, o_hbm, p_ref, o_ref, in_sems, out_sems):
    pairs, rows, width = p_ref.shape
    cols, depth = o_ref.shape[-1] // 2, rows // 2
    blk_count = o_ref.shape[1] // 2
    arrive = [pltpu.make_async_copy(p_hbm.at[g], p_ref.at[g], in_sems.at[g]) for g in range(pairs)]
    leave = [pltpu.make_async_copy(o_ref.at[g], o_hbm.at[g], out_sems.at[g]) for g in range(pairs)]
    for copy in arrive:
        copy.start()
    for g in range(pairs):
        arrive[g].wait()
        for c in range(2):
            own = p_ref[g, c * depth : (c + 1) * depth, :]
            other = p_ref[g, (1 - c) * depth : (2 - c) * depth, :]
            for j in range(blk_count):
                k = (c * blk_count + j) * cols
                o_ref[g, c * blk_count + j] = jnp.concatenate(
                    [own[:, k : k + cols], other[:, k : k + cols]], axis=1
                )
        leave[g].start()
    for copy in leave:
        copy.wait()


def make_slabs(projector, pairs, blk_count, out_rows):
    width = projector.shape[-1]
    p3 = projector.reshape(pairs, -1, width)
    depth = p3.shape[1] // 2
    spread = width // (2 * blk_count * out_rows)
    shape = (pairs, 2 * blk_count, depth, 2 * spread * out_rows)
    if depth % 16 or shape[3] % 128 or spread != 1:
        split = p3.reshape(pairs, 2, depth, spread, 2, blk_count, out_rows)
        split = jnp.stack([split[:, :, :, :, 0], split[:, ::-1, :, :, 1]], axis=1)
        return split.transpose(0, 1, 5, 3, 2, 4, 6).reshape(shape)
    in_hbm = pl.BlockSpec(memory_space=pltpu.HBM)
    return pl.pallas_call(
        slab_kernel,
        out_shape=jax.ShapeDtypeStruct(shape, p3.dtype),
        in_specs=[in_hbm],
        out_specs=in_hbm,
        scratch_shapes=[
            pltpu.VMEM(p3.shape, p3.dtype),
            pltpu.VMEM(shape, p3.dtype),
            pltpu.SemaphoreType.DMA((pairs,)),
            pltpu.SemaphoreType.DMA((pairs,)),
        ],
    )(p3)


def exponent_of(largest):
    return jnp.round(jnp.log2(jnp.clip(largest, 2.0**-100, 2.0**100)))


def fold_kernel(sector_count, out_rows, blk_ref, lane_ref, slab_ref, *refs):
    edge_refs, out_ref, total_ref = refs[:-2], refs[-2], refs[-1]
    peers, blk_count, _, cols = slab_ref.shape
    cols = cols // 2
    order = [lax.rem(blk_ref[0] + blk_count - k, blk_count) for k in range(blk_count)]
    for d in range(peers):
        left = jnp.concatenate([slab_ref[d, j] for j in order], axis=0).T
        left = jnp.concatenate([left[:cols], left[cols:]], axis=1)
        lane = lane_ref[d]
        rows = []
        for b in range(sector_count):
            chosen = (lane == b).astype(jnp.float32).astype(left.dtype)
            rows.append(left * chosen)
        right = jnp.concatenate([e[d] for e in edge_refs], axis=0)
        part = jnp.dot(jnp.concatenate(rows, axis=0), right, preferred_element_type=jnp.float32)
        if d == 0:
            total_ref[...] = part
        else:
            total_ref[...] += part
    exponent = exponent_of(jnp.max(jnp.abs(total_ref[...]), axis=(0, 1), keepdims=True))
    scale = jnp.exp2(TOP - exponent)
    lanes = out_ref.shape[2]
    parts = total_ref.shape[1] // lanes
    dests = out_ref.shape[0]
    for n in range(dests):
        place = (n + dests // 2) % dests
        for k in range(parts):
            out_ref[place, k * out_rows : (k + 1) * out_rows] = (
                total_ref[n * out_rows : (n + 1) * out_rows, k * lanes : (k + 1) * lanes] * scale
            )
        out_ref[place, parts * out_rows :] = jnp.broadcast_to(exponent, (NOTE_ROWS, lanes))


def fold_tiles(slabs, edges, lanes, my_blk, sector_count, out_rows):
    peers, blk_count, depth, cols = slabs.shape
    cols = cols // 2
    width = edges[0].shape[2]
    dests = sector_count * cols // out_rows
    part_width = 128 if width % 128 == 0 else width
    parts = width // part_width
    shape = (dests, parts * out_rows + NOTE_ROWS, part_width)
    if depth * blk_count % 128 or depth % 16 or cols % 64 or out_rows % 16:
        order = (my_blk - jnp.arange(blk_count)) % blk_count
        left = jnp.take(slabs, order, axis=1).reshape(peers, blk_count, depth, 2, cols)
        left = left.transpose(0, 4, 3, 1, 2).reshape(peers, 1, cols, 2 * blk_count * depth)
        labels = jnp.arange(sector_count, dtype=jnp.int32)[None, :, None, None]
        left = left * (lanes[:, :, None, :] == labels).astype(left.dtype)
        right = jnp.concatenate(edges, axis=1)
        total = jnp.einsum("dbsk,dku->bsu", left, right, preferred_element_type=jnp.float32)
        exponent = exponent_of(jnp.max(jnp.abs(total)))
        total = total.reshape(dests, out_rows, parts, part_width) * jnp.exp2(TOP - exponent)
        total = jnp.swapaxes(total, 1, 2).reshape(dests, parts * out_rows, part_width)
        note = jnp.full((dests, NOTE_ROWS, part_width), exponent)
        return jnp.roll(jnp.concatenate([total, note], axis=1), dests // 2, axis=0)
    in_vmem = pl.BlockSpec(memory_space=pltpu.VMEM)
    return pl.pallas_call(
        functools.partial(fold_kernel, sector_count, out_rows),
        out_shape=jax.ShapeDtypeStruct(shape, jnp.float32),
        in_specs=[pl.BlockSpec(memory_space=pltpu.SMEM)] + [in_vmem] * (2 + len(edges)),
        out_specs=in_vmem,
        scratch_shapes=[pltpu.VMEM((sector_count * cols, width), jnp.float32)],
        compiler_params=pltpu.CompilerParams(vmem_limit_bytes=VMEM_LIMIT),
    )(my_blk.reshape(1), lanes, slabs, *edges)


def local(corner, edge_tiles, projector, sector_of):
    sec_count, blk_count = lax.axis_size("sec"), lax.axis_size("blk")
    me, my_blk = lax.axis_index("sec"), lax.axis_index("blk")
    tile_count, tile_rows, width = edge_tiles.shape
    columns = sec_count // 2
    per_peer = tile_count // sec_count
    slab_depth = per_peer * tile_rows
    corner_rows = corner.shape[0]
    sector_count = corner_rows * sec_count // width
    out_rows = corner_rows // blk_count
    spread = columns // sector_count
    sibling = [(i, i ^ 1) for i in range(sec_count)]

    def turn(array, by):
        return lax.ppermute(array, "blk", [(j, (j + by) % blk_count) for j in range(blk_count)])

    edges3 = edge_tiles.reshape(sec_count, slab_depth, width)
    edge_turns = [edges3] + [turn(edges3, k) for k in range(1, blk_count)]
    sectors = jnp.stack([sector_of] + [turn(sector_of, k) for k in range(1, blk_count)])
    lanes = jnp.stack([sectors, lax.ppermute(sectors, "sec", sibling)])
    lanes = jnp.moveaxis(lanes.reshape(2 * blk_count, sec_count, per_peer), 1, 0)
    lanes = jnp.repeat(lanes.reshape(sec_count, 1, -1), tile_rows, axis=2)
    others = [lax.ppermute(edges3, "sec", sibling)]
    edge_turns, lanes = lax.optimization_barrier((edge_turns, lanes))
    others += [lax.ppermute(e, "sec", sibling) for e in edge_turns[1:]]

    slabs = make_slabs(projector, columns, blk_count, out_rows)
    slabs = slabs.reshape(sec_count * blk_count, slab_depth, 2 * spread * out_rows)
    arrived = lax.all_to_all(slabs, ("sec", "blk"), split_axis=0, concat_axis=0, tiled=True)
    arrived = arrived.reshape(sec_count, blk_count, slab_depth, 2 * spread * out_rows)

    partial = fold_tiles(arrived, edge_turns + others, lanes, my_blk, sector_count, out_rows)
    middle = [(n - columns // 2) % columns for n in range(columns)]
    groups = [[2 * n + c for n in middle] for c in range(2)]
    received = lax.all_to_all(
        partial.astype(jnp.float16),
        "sec",
        split_axis=0,
        concat_axis=0,
        tiled=True,
        axis_index_groups=groups,
    ).astype(jnp.float32)
    scales = jnp.exp2(received[:, -1:, :1] - TOP)
    rows = jnp.sum(received[:, :-NOTE_ROWS] * scales, axis=0)
    rows = jnp.concatenate(jnp.split(rows, rows.shape[0] // out_rows), axis=1)

    share = 2 * spread
    place = me % share
    block = jnp.zeros((share, corner_rows, width), corner.dtype)
    for k in range(share):
        ring = [(i, i // share * share + (i % share + k) % share) for i in range(sec_count)]
        piece = corner if k == 0 else lax.ppermute(corner, "sec", ring)
        block = lax.dynamic_update_index_in_dim(block, piece, (place - k) % share, 0)
    block = block.reshape(width, width)
    high = lax.reduce_precision(rows, exponent_bits=8, mantissa_bits=7)
    both = jnp.concatenate([high, rows - high], axis=0).astype(jnp.bfloat16)
    both = jnp.dot(both, block, preferred_element_type=jnp.float32)
    return both[:out_rows] + both[out_rows:]


def solution(mesh):
    in_specs = (
        P("sec", None),
        P(("sec", "blk"), None, None),
        P(("sec", "blk"), None, None),
        P(("sec", "blk")),
    )
    out_specs = P(("sec", "blk"), None)
    return jax.shard_map(local, mesh=mesh, in_specs=in_specs, out_specs=out_specs, check_vma=False)
```

time: 49.2 us -> 41.7 us (0.85)
  waiting for transfers between devices: 24.7 us -> 18.9 us
  local copies, waits for them, and re-layouts: 3.76 us -> 0.52 us
  starting transfers between devices: 14.6 us -> 16.1 us
  Pallas kernels: 3.03 us -> 3.74 us
  other arithmetic: 2.36 us -> 1.71 us
    all_to_all x1, waiting for transfers between devices: 13.6 us -> 5.84 us  [local(): lax.all_to_all(partial.astype(jnp.float16), 'sec', split_axis=0, concat_a...]
    unnamed x14 -> x6, local copies, waits for them, and re-layouts: 2.65 us -> 0.02 us
    select_n x3 -> x0, other arithmetic: 1.56 us -> none  [the longest x1 1.53 us: pairwise(): return (jnp.where(odd, second, first), jnp.where(odd, first, second))]
    ppermute x2, starting transfers between devices: 3.61 us -> 4.8 us  [turn(): lax.ppermute(array, 'blk', [(j, (j + by) % blk_count) for j in range(blk_...]
    ppermute x2, waiting for transfers between devices: 5.52 us -> 6.6 us  [turn(): lax.ppermute(array, 'blk', [(j, (j + by) % blk_count) for j in range(blk_...]
    all_to_all x1, starting transfers between devices: 4.58 us -> 5.64 us  [local(): lax.all_to_all(partial.astype(jnp.float16), 'sec', split_axis=0, concat_a...]
    all_to_all x1, starting transfers between devices: 5.71 us -> 4.9 us  [local(): lax.all_to_all(slabs, ('sec', 'blk'), split_axis=0, concat_axis=0, tiled=...]
    convert_element_type x1 -> x2, other arithmetic: 0.01 us -> 0.79 us  [the longest x1 0.75 us: local(): partial.astype(jnp.float16)]
  transfers between devices with their start and end apart: 8 -> 8, of which waited for: 5 -> 6; matrix products, arithmetic and copies ran while one was open for 6% -> 1% of each run, Pallas kernels for 2% -> 6%
where the time goes in v2:
time: 41.7 us; the launch traced here: 41.3 us
  waiting for transfers between devices  18.9 us (45%)
  starting transfers between devices  16.1 us (39%)
  Pallas kernels  3.74 us (9%)
  other arithmetic  1.71 us (4%)
  local copies, waits for them, and re-layouts  0.52 us (1%)
    ppermute x2, waiting for transfers between devices, turn(): lax.ppermute(array, 'blk', [(j, (j + by) % blk_count) for j in range(blk_...  6.6 us
    all_to_all x1, waiting for transfers between devices, local(): lax.all_to_all(partial.astype(jnp.float16), 'sec', split_axis=0, concat_a...  5.84 us
    all_to_all x1, starting transfers between devices, local(): lax.all_to_all(partial.astype(jnp.float16), 'sec', split_axis=0, concat_a...  5.64 us
    all_to_all x1, starting transfers between devices, local(): lax.all_to_all(slabs, ('sec', 'blk'), split_axis=0, concat_axis=0, tiled=...  4.9 us
    ppermute x2, starting transfers between devices, turn(): lax.ppermute(array, 'blk', [(j, (j + by) % blk_count) for j in range(blk_...  4.8 us
    all_to_all x1, waiting for transfers between devices, local(): lax.all_to_all(slabs, ('sec', 'blk'), split_axis=0, concat_axis=0, tiled=...  4.5 us
    pallas_call x1, Pallas kernels, make_slabs(): pl.pallas_call(slab_kernel, out_shape=jax.ShapeDtypeStruct(shape, p3.dtyp...  2.3 us
    pallas_call x1, Pallas kernels, fold_tiles(): pl.pallas_call(functools.partial(fold_kernel, sector_count, out_rows), ou...  1.44 us
  transfers between devices with their start and end apart: 8, of which 6 were waited for; matrix products, arithmetic and copies ran while one was open for 1% of the time, Pallas kernels for 6%

profile of v2, /device:TPU:0, one launch (start us, length us, event | category | flops | bytes accessed | tf_op | source)
XLA Modules:
  0.0 41.3 jit_solution(7596944735099659041)
XLA Ops:
  0.0 3.0 %collective-permute-start = (bf16[16,64,256]{2,1,0:T(8,128)(2,1)}, bf16[16,64,256]{2,1,0:T(8,128)(2,1)S(1)}, u32[]{:S(2)}, u32[]{:S(2)}) collective-permute-start(bf16[16,64,256]{2,1,0:T(8,128)(2,1)} %bitcast.19), channel_id=1, source_target_pairs={{0,1},{1,0},{2,3},{3,2},{4,5},{5,4},{6,7},{7,6},{8,9},{9,8},{10,11... | collective-permute-start | bytes 1572872 | tf_op jit(solution)/shard_map/ppermute | solution.py:146
  3.0 2.3 %shard_map.46 = bf16[8,4,64,128]{3,2,1,0:T(8,128)(2,1)} custom-call(bf16[8,128,256]{2,1,0:T(8,128)(2,1)} %bitcast.23), custom_call_target="tpu_custom_call" | custom-call | tf_op jit(solution)/shard_map/pallas_call | solution.py:49
  5.3 0.0 copy-start.2
  5.3 0.0 copy-start
  5.3 4.9 %all-to-all-start = ((bf16[32,64,128]{2,1,0:T(8,128)(2,1)}), bf16[32,64,128]{2,1,0:T(8,128)(2,1)S(1)}, u32[]{:S(2)}, u32[]{:S(2)}) async-start(bf16[32,64,128]{2,1,0:T(8,128)(2,1)} %bitcast.22), calls=%async_computation | async-start | bytes 1048576 | tf_op jit(solution)/shard_map/all_to_all | solution.py:160
  10.2 0.0 copy-done.2
  10.2 1.8 %collective-permute-start.1 = (s32[64]{0:T(128)S(1)}, s32[64]{0:T(128)S(1)}, u32[]{:S(2)}, u32[]{:S(2)}) collective-permute-start(s32[64]{0:T(128)S(1)} %copy-done.2), channel_id=1, source_target_pairs={{0,1},{1,0},{2,3},{3,2},{4,5},{5,4},{6,7},{7,6},{8,9},{9,8},{10,11... | collective-permute-start | bytes 776 | tf_op jit(solution)/shard_map/ppermute | solution.py:146
  12.1 6.6 %collective-permute-done.1 = s32[64]{0:T(128)S(1)} collective-permute-done((s32[64]{0:T(128)S(1)}, s32[64]{0:T(128)S(1)}, u32[]{:S(2)}, u32[]{:S(2)}) %collective-permute-start.1) | collective-permute-done | bytes 288 | tf_op jit(solution)/shard_map/ppermute | solution.py:146
  18.7 0.0 collective-permute-start.2
  18.7 0.0 copy-done
  18.7 0.5 %collective-permute-start.3 = (bf16[16,64,256]{2,1,0:T(8,128)(2,1)S(1)}, bf16[16,64,256]{2,1,0:T(8,128)(2,1)S(1)}, u32[]{:S(2)}, u32[]{:S(2)}) collective-permute-start(bf16[16,64,256]{2,1,0:T(8,128)(2,1)S(1)} %bitcast.20), channel_id=1, source_target_pairs={{0,2},{2,0},{4,6},{6,4},{8,10},{10,8},{12,14},{14,12},{16,18},{18,... | collective-permute-start | bytes 1572872 | tf_op jit(solution)/shard_map/ppermute | solution.py:154
  19.2 0.6 %collective-permute-done.2 = s32[2,64]{1,0:T(2,128)S(1)} collective-permute-done((s32[2,64]{1,0:T(2,128)S(1)}, s32[2,64]{1,0:T(2,128)S(1)}, u32[]{:S(2)}, u32[]{:S(2)}) %collective-permute-start.2) | collective-permute-done | bytes 544 | tf_op jit(solution)/shard_map/ppermute | solution.py:151
  19.8 0.1 reshape.32
  19.9 0.1 copy.5
  20.0 0.1 copy.6
  20.1 0.1 broadcast_in_dim.15
  20.2 0.1 broadcast_in_dim.16.lane_ref
  20.3 0.0 collective-permute-done.refs_1_
  20.3 0.3 collective-permute-start.4
  20.6 0.1 collective-permute-done.3.refs_2_
  20.7 4.5 %all-to-all-done = bf16[32,64,128]{2,1,0:T(8,128)(2,1)S(1)} async-done(((bf16[32,64,128]{2,1,0:T(8,128)(2,1)}), bf16[32,64,128]{2,1,0:T(8,128)(2,1)S(1)}, u32[]{:S(2)}, u32[]{:S(2)}) %all-to-all-start) | async-done | bytes 524320 | tf_op jit(solution)/shard_map/all_to_all | solution.py:160
  25.2 0.0 collective-permute-done.4.refs_3_
  25.2 1.4 %shard_map.47 = f32[8,136,128]{2,1,0:T(8,128)S(1)} custom-call(s32[1]{0:T(128)} %bitcast.blk_ref, s32[16,1,256]{2,1,0:T(1,128)S(1)} %broadcast_in_dim.16.lane_ref, bf16[16,2,64,128]{3,2,1,0:T(8,128)(2,1)S(1)} %bitcast.18, bf16[16,64,256]{2,1,0:T(8,128)(2,1)S(1)} %bitcast.21, bf16[16,64,256]{2,1,0:T(8,128)(2,1)S(1)} %collective-permute-done.refs_1_, ...), custom_call_target="tpu_custom_call" | custom-call | tf_op jit(solution)/shard_map/pallas_call | solution.py:122
  26.7 0.8 %convert_element_type.7 = f16[8,136,128]{2,1,0:T(8,128)(2,1)} convert(f32[8,136,128]{2,1,0:T(8,128)S(1)} %shard_map.47) | non-fusion elementwise | flops 139264 | bytes 835584 | tf_op jit(solution)/shard_map/convert_element_type | solution.py:167
  27.4 0.0 copy-start.1
  27.4 5.6 %all-to-all-start.1 = ((f16[8,136,128]{2,1,0:T(8,128)(2,1)}), f16[8,136,128]{2,1,0:T(8,128)(2,1)S(1)}, u32[]{:S(2)}, u32[]{:S(2)}) async-start(f16[8,136,128]{2,1,0:T(8,128)(2,1)} %convert_element_type.7), calls=%async_computation.1 | async-start | bytes 557056 | tf_op jit(solution)/shard_map/all_to_all | solution.py:166
  33.1 0.0 copy-done.1
  33.1 0.0 collective-permute-start.5
  33.2 1.2 %collective-permute-done.5 = bf16[128,256]{1,0:T(8,128)(2,1)S(1)} collective-permute-done((bf16[128,256]{1,0:T(8,128)(2,1)S(1)}, bf16[128,256]{1,0:T(8,128)(2,1)S(1)}, u32[]{:S(2)}, u32[]{:S(2)}) %collective-permute-start.5) | collective-permute-done | bytes 65568 | tf_op jit(solution)/shard_map/ppermute | solution.py:183
  34.3 5.8 %all-to-all-done.1 = f16[8,136,128]{2,1,0:T(8,128)(2,1)S(1)} async-done(((f16[8,136,128]{2,1,0:T(8,128)(2,1)}), f16[8,136,128]{2,1,0:T(8,128)(2,1)S(1)}, u32[]{:S(2)}, u32[]{:S(2)}) %all-to-all-start.1) | async-done | bytes 278560 | tf_op jit(solution)/shard_map/all_to_all | solution.py:166
  40.2 0.2 fusion.8
  40.4 0.1 fusion
  40.5 0.2 fusion.2
  40.7 0.6 %slice_add_fusion = f32[64,256]{1,0:T(8,128)} fusion(f32[128,256]{1,0:T(8,128)S(1)} %fusion.2), kind=kLoop, calls=%fused_computation.5 | loop fusion | flops 16384 | bytes 196608 | tf_op jit(solution)/shard_map/add | solution.py:189
  (8 shorter events, 0.1 us)
Async XLA Ops:
  0.0 20.3 %collective-permute-start = (bf16[16,64,256]{2,1,0:T(8,128)(2,1)}, bf16[16,64,256]{2,1,0:T(8,128)(2,1)S(1)}, u32[]{:S(2)}, u32[]{:S(2)}) collective-permute-start(bf16[16,64,256]{2,1,0:T(8,128)(2,1)} %bitcast.19), channel_id=1, source_target_pairs={{0,1},{1,0},{2,3},{3,2},{4,5},{5,4},{6,7},{7,6},{8,9},{9,8},{10,11... | collective-permute-start | bytes 1572872 | tf_op jit(solution)/shard_map/ppermute | solution.py:146
  5.3 4.9 %copy-start.2 = (s32[64]{0:T(128)S(1)}, s32[64]{0:T(128)}, u32[]{:S(2)}) copy-start(s32[64]{0:T(128)} %param.7) | copy-start | bytes 772
  5.3 13.4 %copy-start = (bf16[64,16,256]{2,1,0:T(8,128)(2,1)S(1)}, bf16[64,16,256]{2,1,0:T(8,128)(2,1)}, u32[]{:S(2)}) copy-start(bf16[64,16,256]{2,1,0:T(8,128)(2,1)} %param.5) | copy-start | bytes 1572868
  5.3 19.9 %all-to-all-start = ((bf16[32,64,128]{2,1,0:T(8,128)(2,1)}), bf16[32,64,128]{2,1,0:T(8,128)(2,1)S(1)}, u32[]{:S(2)}, u32[]{:S(2)}) async-start(bf16[32,64,128]{2,1,0:T(8,128)(2,1)} %bitcast.22), calls=%async_computation | async-start | bytes 1048576 | tf_op jit(solution)/shard_map/all_to_all | solution.py:160
  10.2 8.4 %collective-permute-start.1 = (s32[64]{0:T(128)S(1)}, s32[64]{0:T(128)S(1)}, u32[]{:S(2)}, u32[]{:S(2)}) collective-permute-start(s32[64]{0:T(128)S(1)} %copy-done.2), channel_id=1, source_target_pairs={{0,1},{1,0},{2,3},{3,2},{4,5},{5,4},{6,7},{7,6},{8,9},{9,8},{10,11... | collective-permute-start | bytes 776 | tf_op jit(solution)/shard_map/ppermute | solution.py:146
  18.7 1.1 %collective-permute-start.2 = (s32[2,64]{1,0:T(2,128)S(1)}, s32[2,64]{1,0:T(2,128)S(1)}, u32[]{:S(2)}, u32[]{:S(2)}) collective-permute-start(s32[2,64]{1,0:T(2,128)S(1)} %get-tuple-element.16), channel_id=1, source_target_pairs={{0,2},{2,0},{4,6},{6,4},{8,10},{10,8},{12,14},{14,12},{16,18},{18,... | collective-permute-start | bytes 1544 | tf_op jit(solution)/shard_map/ppermute | solution.py:151
  18.7 2.0 %collective-permute-start.3 = (bf16[16,64,256]{2,1,0:T(8,128)(2,1)S(1)}, bf16[16,64,256]{2,1,0:T(8,128)(2,1)S(1)}, u32[]{:S(2)}, u32[]{:S(2)}) collective-permute-start(bf16[16,64,256]{2,1,0:T(8,128)(2,1)S(1)} %bitcast.20), channel_id=1, source_target_pairs={{0,2},{2,0},{4,6},{6,4},{8,10},{10,8},{12,14},{14,12},{16,18},{18,... | collective-permute-start | bytes 1572872 | tf_op jit(solution)/shard_map/ppermute | solution.py:154
  20.3 4.9 %collective-permute-start.4 = (bf16[16,64,256]{2,1,0:T(8,128)(2,1)S(1)}, bf16[16,64,256]{2,1,0:T(8,128)(2,1)S(1)}, u32[]{:S(2)}, u32[]{:S(2)}) collective-permute-start(bf16[16,64,256]{2,1,0:T(8,128)(2,1)S(1)} %collective-permute-done.refs_1_), channel_id=1, source_target_pairs={{0,2},{2,0},{4,6},{6,4},{8,10},{10,8},{12,14},{14,12},{16,18},{18,... | collective-permute-start | bytes 1572872 | tf_op jit(solution)/shard_map/ppermute | solution.py:156
  27.4 5.6 %copy-start.1 = (bf16[128,256]{1,0:T(8,128)(2,1)S(1)}, bf16[128,256]{1,0:T(8,128)(2,1)}, u32[]{:S(2)}) copy-start(bf16[128,256]{1,0:T(8,128)(2,1)} %param.4) | copy-start | bytes 196612
  27.4 12.8 %all-to-all-start.1 = ((f16[8,136,128]{2,1,0:T(8,128)(2,1)}), f16[8,136,128]{2,1,0:T(8,128)(2,1)S(1)}, u32[]{:S(2)}, u32[]{:S(2)}) async-start(f16[8,136,128]{2,1,0:T(8,128)(2,1)} %convert_element_type.7), calls=%async_computation.1 | async-start | bytes 557056 | tf_op jit(solution)/shard_map/all_to_all | solution.py:166
  33.1 1.3 %collective-permute-start.5 = (bf16[128,256]{1,0:T(8,128)(2,1)S(1)}, bf16[128,256]{1,0:T(8,128)(2,1)S(1)}, u32[]{:S(2)}, u32[]{:S(2)}) collective-permute-start(bf16[128,256]{1,0:T(8,128)(2,1)S(1)} %copy-done.1), channel_id=1, source_target_pairs={{0,2},{2,0},{4,6},{6,4},{8,10},{10,8},{12,14},{14,12},{16,18},{18,... | collective-permute-start | bytes 196616 | tf_op jit(solution)/shard_map/ppermute | solution.py:183

commit v3 on v2

--- a/solution.py
+++ b/solution.py
@@ -2,6 +2,7 @@
 
 import jax
 import jax.numpy as jnp
+import numpy as np
 from jax import lax
 from jax.experimental import pallas as pl
 from jax.experimental.pallas import tpu as pltpu
@@ -12,25 +13,32 @@
 NOTE_ROWS = 8
 
 
+def ring_of(count):
+    stride = 3 if count % 3 else 1
+    return [-stride * n % count for n in range(count)]
+
+
 def slab_kernel(p_hbm, o_hbm, p_ref, o_ref, in_sems, out_sems):
-    pairs, rows, width = p_ref.shape
-    cols, depth = o_ref.shape[-1] // 2, rows // 2
-    blk_count = o_ref.shape[1] // 2
-    arrive = [pltpu.make_async_copy(p_hbm.at[g], p_ref.at[g], in_sems.at[g]) for g in range(pairs)]
-    leave = [pltpu.make_async_copy(o_ref.at[g], o_hbm.at[g], out_sems.at[g]) for g in range(pairs)]
+    pairs = p_ref.shape[0]
+    dests, depth, cols = o_ref.shape
+    per_pair, cols = dests // pairs, cols // 2
+    parts = [pl.ds(h * pairs // 2, pairs // 2) for h in range(2)]
+    arrive = [pltpu.make_async_copy(p_hbm.at[h], p_ref.at[h], in_sems.at[k]) for k, h in enumerate(parts)]
+    parts = [pl.ds(h * dests // 2, dests // 2) for h in range(2)]
+    leave = [pltpu.make_async_copy(o_ref.at[h], o_hbm.at[h], out_sems.at[k]) for k, h in enumerate(parts)]
     for copy in arrive:
         copy.start()
-    for g in range(pairs):
-        arrive[g].wait()
-        for c in range(2):
-            own = p_ref[g, c * depth : (c + 1) * depth, :]
-            other = p_ref[g, (1 - c) * depth : (2 - c) * depth, :]
-            for j in range(blk_count):
-                k = (c * blk_count + j) * cols
-                o_ref[g, c * blk_count + j] = jnp.concatenate(
-                    [own[:, k : k + cols], other[:, k : k + cols]], axis=1
-                )
-        leave[g].start()
+    for copy in arrive:
+        copy.wait()
+    for place, n in enumerate(ring_of(dests)):
+        g, j = divmod(n, per_pair)
+        c = 2 * j // per_pair
+        own = p_ref[g, c * depth : (c + 1) * depth, j * cols : (j + 1) * cols]
+        other = p_ref[g, (1 - c) * depth : (2 - c) * depth, j * cols : (j + 1) * cols]
+        o_ref[place] = jnp.concatenate([own, other], axis=1)
+        if place + 1 == dests // 2:
+            leave[0].start()
+    leave[1].start()
     for copy in leave:
         copy.wait()
 
@@ -40,11 +48,13 @@
     p3 = projector.reshape(pairs, -1, width)
     depth = p3.shape[1] // 2
     spread = width // (2 * blk_count * out_rows)
-    shape = (pairs, 2 * blk_count, depth, 2 * spread * out_rows)
-    if depth % 16 or shape[3] % 128 or spread != 1:
+    dests = pairs * 2 * blk_count
+    shape = (dests, depth, 2 * spread * out_rows)
+    if depth % 16 or shape[2] % 128 or spread != 1 or pairs % 2:
         split = p3.reshape(pairs, 2, depth, spread, 2, blk_count, out_rows)
         split = jnp.stack([split[:, :, :, :, 0], split[:, ::-1, :, :, 1]], axis=1)
-        return split.transpose(0, 1, 5, 3, 2, 4, 6).reshape(shape)
+        slabs = split.transpose(0, 1, 5, 3, 2, 4, 6).reshape(shape)
+        return jnp.take(slabs, np.array(ring_of(dests)), axis=0)
     in_hbm = pl.BlockSpec(memory_space=pltpu.HBM)
     return pl.pallas_call(
         slab_kernel,
@@ -54,8 +64,8 @@
         scratch_shapes=[
             pltpu.VMEM(p3.shape, p3.dtype),
             pltpu.VMEM(shape, p3.dtype),
-            pltpu.SemaphoreType.DMA((pairs,)),
-            pltpu.SemaphoreType.DMA((pairs,)),
+            pltpu.SemaphoreType.DMA((2,)),
+            pltpu.SemaphoreType.DMA((2,)),
         ],
     )(p3)
 
@@ -66,11 +76,20 @@
 
 def fold_kernel(sector_count, out_rows, blk_ref, lane_ref, slab_ref, *refs):
     edge_refs, out_ref, total_ref = refs[:-2], refs[-2], refs[-1]
-    peers, blk_count, _, cols = slab_ref.shape
-    cols = cols // 2
+    peers = lane_ref.shape[0]
+    sources, _, cols = slab_ref.shape
+    cols, blk_count = cols // 2, sources // peers
+    place = {n: k for k, n in enumerate(ring_of(sources))}
     order = [lax.rem(blk_ref[0] + blk_count - k, blk_count) for k in range(blk_count)]
     for d in range(peers):
-        left = jnp.concatenate([slab_ref[d, j] for j in order], axis=0).T
+        places = [place[d * blk_count + j] for j in range(blk_count)]
+        left = []
+        for j in order:
+            n = places[0]
+            for k in range(1, blk_count):
+                n = jnp.where(j == k, places[k], n)
+            left.append(slab_ref[n])
+        left = jnp.concatenate(left, axis=0).T
         left = jnp.concatenate([left[:cols], left[cols:]], axis=1)
         lane = lane_ref[d]
         rows = []
@@ -98,16 +117,18 @@
 
 
 def fold_tiles(slabs, edges, lanes, my_blk, sector_count, out_rows):
-    peers, blk_count, depth, cols = slabs.shape
-    cols = cols // 2
-    width = edges[0].shape[2]
+    sources, depth, cols = slabs.shape
+    peers, _, width = edges[0].shape
+    cols, blk_count = cols // 2, sources // peers
     dests = sector_count * cols // out_rows
     part_width = 128 if width % 128 == 0 else width
     parts = width // part_width
     shape = (dests, parts * out_rows + NOTE_ROWS, part_width)
     if depth * blk_count % 128 or depth % 16 or cols % 64 or out_rows % 16:
         order = (my_blk - jnp.arange(blk_count)) % blk_count
-        left = jnp.take(slabs, order, axis=1).reshape(peers, blk_count, depth, 2, cols)
+        left = jnp.take(slabs, np.argsort(ring_of(sources)), axis=0)
+        left = left.reshape(peers, blk_count, depth, 2, cols)
+        left = jnp.take(left, order, axis=1)
         left = left.transpose(0, 4, 3, 1, 2).reshape(peers, 1, cols, 2 * blk_count * depth)
         labels = jnp.arange(sector_count, dtype=jnp.int32)[None, :, None, None]
         left = left * (lanes[:, :, None, :] == labels).astype(left.dtype)
@@ -156,9 +177,14 @@
     others += [lax.ppermute(e, "sec", sibling) for e in edge_turns[1:]]
 
     slabs = make_slabs(projector, columns, blk_count, out_rows)
-    slabs = slabs.reshape(sec_count * blk_count, slab_depth, 2 * spread * out_rows)
-    arrived = lax.all_to_all(slabs, ("sec", "blk"), split_axis=0, concat_axis=0, tiled=True)
-    arrived = arrived.reshape(sec_count, blk_count, slab_depth, 2 * spread * out_rows)
+    arrived = lax.all_to_all(
+        slabs,
+        ("sec", "blk"),
+        split_axis=0,
+        concat_axis=0,
+        tiled=True,
+        axis_index_groups=[ring_of(sec_count * blk_count)],
+    )
 
     partial = fold_tiles(arrived, edge_turns + others, lanes, my_blk, sector_count, out_rows)
     middle = [(n - columns // 2) % columns for n in range(columns)]
@@ -184,9 +210,9 @@
         block = lax.dynamic_update_index_in_dim(block, piece, (place - k) % share, 0)
     block = block.reshape(width, width)
     high = lax.reduce_precision(rows, exponent_bits=8, mantissa_bits=7)
-    both = jnp.concatenate([high, rows - high], axis=0).astype(jnp.bfloat16)
-    both = jnp.dot(both, block, preferred_element_type=jnp.float32)
-    return both[:out_rows] + both[out_rows:]
+    both = jnp.concatenate([high, rows - high], axis=1).astype(jnp.bfloat16)
+    twice = jnp.concatenate([block, block], axis=0)
+    return jnp.dot(both, twice, preferred_element_type=jnp.float32)
 
 
 def solution(mesh):

time: 41.7 us -> 40.7 us (0.976)
  matrix products: 0.16 us -> 0.8 us
  other arithmetic: 1.71 us -> 1.07 us
  waiting for transfers between devices: 18.9 us -> 18.4 us
    all_to_all x1, waiting for transfers between devices: 4.5 us -> 3.31 us  [local(): lax.all_to_all(slabs, ('sec', 'blk'), split_axis=0, concat_axis=0, tiled=...]
    ppermute x2, waiting for transfers between devices: 6.6 us -> 7.73 us  [turn(): lax.ppermute(array, 'blk', [(j, (j + by) % blk_count) for j in range(blk_...]
    dot_general x1, matrix products: 0.16 us -> 0.8 us  [local(): return jnp.dot(both, twice, preferred_element_type=jnp.float32)]
    add x1 -> x0, other arithmetic: 0.64 us -> none  [local(): return both[:out_rows] + both[out_rows:]]
    all_to_all x1, waiting for transfers between devices: 5.84 us -> 5.38 us  [local(): lax.all_to_all(partial.astype(jnp.float16), 'sec', split_axis=0, concat_a...]
  transfers between devices with their start and end apart: 8 -> 8, of which waited for: 6 -> 6; matrix products, arithmetic and copies ran while one was open for 1% -> 1% of each run, Pallas kernels for 6% -> 5%
where the time goes in v3:
time: 40.7 us; the launch traced here: 40.3 us
  waiting for transfers between devices  18.4 us (45%)
  starting transfers between devices  15.9 us (39%)
  Pallas kernels  3.43 us (8%)
  other arithmetic  1.07 us (3%)
  matrix products  0.8 us (2%)
  local copies, waits for them, and re-layouts  0.52 us (1%)
    ppermute x2, waiting for transfers between devices, turn(): lax.ppermute(array, 'blk', [(j, (j + by) % blk_count) for j in range(blk_...  7.73 us
    all_to_all x1, starting transfers between devices, local(): lax.all_to_all(partial.astype(jnp.float16), 'sec', split_axis=0, concat_a...  5.43 us
    all_to_all x1, waiting for transfers between devices, local(): lax.all_to_all(partial.astype(jnp.float16), 'sec', split_axis=0, concat_a...  5.38 us
    all_to_all x1, starting transfers between devices, local(): lax.all_to_all(slabs, ('sec', 'blk'), split_axis=0, concat_axis=0, tiled=...  4.9 us
    ppermute x2, starting transfers between devices, turn(): lax.ppermute(array, 'blk', [(j, (j + by) % blk_count) for j in range(blk_...  4.8 us
    all_to_all x1, waiting for transfers between devices, local(): lax.all_to_all(slabs, ('sec', 'blk'), split_axis=0, concat_axis=0, tiled=...  3.31 us
    pallas_call x1, Pallas kernels, make_slabs(): pl.pallas_call(slab_kernel, out_shape=jax.ShapeDtypeStruct(shape, p3.dtyp...  1.99 us
    pallas_call x1, Pallas kernels, fold_tiles(): pl.pallas_call(functools.partial(fold_kernel, sector_count, out_rows), ou...  1.44 us
  transfers between devices with their start and end apart: 8, of which 6 were waited for; matrix products, arithmetic and copies ran while one was open for 1% of the time, Pallas kernels for 5%

profile of v3, /device:TPU:0, one launch (start us, length us, event | category | flops | bytes accessed | tf_op | source)
XLA Modules:
  0.0 40.3 jit_solution(3870797757682766547)
XLA Ops:
  0.0 3.0 %collective-permute-start = (bf16[16,64,256]{2,1,0:T(8,128)(2,1)}, bf16[16,64,256]{2,1,0:T(8,128)(2,1)S(1)}, u32[]{:S(2)}, u32[]{:S(2)}) collective-permute-start(bf16[16,64,256]{2,1,0:T(8,128)(2,1)} %bitcast.15), channel_id=1, source_target_pairs={{0,1},{1,0},{2,3},{3,2},{4,5},{5,4},{6,7},{7,6},{8,9},{9,8},{10,11... | collective-permute-start | bytes 1572872 | tf_op jit(solution)/shard_map/ppermute | solution.py:167
  3.0 2.0 %shard_map.46 = bf16[32,64,128]{2,1,0:T(8,128)(2,1)} custom-call(bf16[8,128,256]{2,1,0:T(8,128)(2,1)} %bitcast.18), custom_call_target="tpu_custom_call" | custom-call | tf_op jit(solution)/shard_map/pallas_call | solution.py:59
  5.0 0.0 copy-start.2
  5.0 0.0 copy-start
  5.0 4.9 %all-to-all-start = ((bf16[32,64,128]{2,1,0:T(8,128)(2,1)}), bf16[32,64,128]{2,1,0:T(8,128)(2,1)S(1)}, u32[]{:S(2)}, u32[]{:S(2)}) async-start(bf16[32,64,128]{2,1,0:T(8,128)(2,1)} %shard_map.46), calls=%async_computation | async-start | bytes 1048576 | tf_op jit(solution)/shard_map/all_to_all | solution.py:180
  9.9 0.0 copy-done.2
  9.9 1.8 %collective-permute-start.1 = (s32[64]{0:T(128)S(1)}, s32[64]{0:T(128)S(1)}, u32[]{:S(2)}, u32[]{:S(2)}) collective-permute-start(s32[64]{0:T(128)S(1)} %copy-done.2), channel_id=1, source_target_pairs={{0,1},{1,0},{2,3},{3,2},{4,5},{5,4},{6,7},{7,6},{8,9},{9,8},{10,11... | collective-permute-start | bytes 776 | tf_op jit(solution)/shard_map/ppermute | solution.py:167
  11.7 7.7 %collective-permute-done.1 = s32[64]{0:T(128)S(1)} collective-permute-done((s32[64]{0:T(128)S(1)}, s32[64]{0:T(128)S(1)}, u32[]{:S(2)}, u32[]{:S(2)}) %collective-permute-start.1) | collective-permute-done | bytes 288 | tf_op jit(solution)/shard_map/ppermute | solution.py:167
  19.5 0.1 collective-permute-start.2
  19.6 0.0 copy-done
  19.6 0.5 %collective-permute-start.3 = (bf16[16,64,256]{2,1,0:T(8,128)(2,1)S(1)}, bf16[16,64,256]{2,1,0:T(8,128)(2,1)S(1)}, u32[]{:S(2)}, u32[]{:S(2)}) collective-permute-start(bf16[16,64,256]{2,1,0:T(8,128)(2,1)S(1)} %bitcast.16), channel_id=1, source_target_pairs={{0,2},{2,0},{4,6},{6,4},{8,10},{10,8},{12,14},{14,12},{16,18},{18,... | collective-permute-start | bytes 1572872 | tf_op jit(solution)/shard_map/ppermute | solution.py:175
  20.1 0.6 %collective-permute-done.2 = s32[2,64]{1,0:T(2,128)S(1)} collective-permute-done((s32[2,64]{1,0:T(2,128)S(1)}, s32[2,64]{1,0:T(2,128)S(1)}, u32[]{:S(2)}, u32[]{:S(2)}) %collective-permute-start.2) | collective-permute-done | bytes 544 | tf_op jit(solution)/shard_map/ppermute | solution.py:172
  20.7 0.1 reshape.26
  20.8 0.1 copy.5
  20.9 0.1 copy.6
  20.9 0.1 broadcast_in_dim.15
  21.1 0.1 broadcast_in_dim.16.lane_ref
  21.2 0.0 collective-permute-done.refs_1_
  21.2 0.3 collective-permute-start.4
  21.4 0.1 collective-permute-done.3.refs_2_
  21.6 3.3 %all-to-all-done.slab_ref = bf16[32,64,128]{2,1,0:T(8,128)(2,1)S(1)} async-done(((bf16[32,64,128]{2,1,0:T(8,128)(2,1)}), bf16[32,64,128]{2,1,0:T(8,128)(2,1)S(1)}, u32[]{:S(2)}, u32[]{:S(2)}) %all-to-all-start) | async-done | bytes 524320 | tf_op jit(solution)/shard_map/all_to_all | solution.py:180
  24.9 0.0 collective-permute-done.4.refs_3_
  24.9 1.4 %shard_map.47 = f32[8,136,128]{2,1,0:T(8,128)S(1)} custom-call(s32[1]{0:T(128)} %bitcast.blk_ref, s32[16,1,256]{2,1,0:T(1,128)S(1)} %broadcast_in_dim.16.lane_ref, bf16[32,64,128]{2,1,0:T(8,128)(2,1)S(1)} %all-to-all-done.slab_ref, bf16[16,64,256]{2,1,0:T(8,128)(2,1)S(1)} %bitcast.17, bf16[16,64,256]{2,1,0:T(8,128)(2,1)S(1)} %collective-permute-done.refs_1_, ...), custom_call_target="tpu_custom_call" | custom-call | tf_op jit(solution)/shard_map/pallas_call | solution.py:143
  26.4 0.8 %convert_element_type.7 = f16[8,136,128]{2,1,0:T(8,128)(2,1)} convert(f32[8,136,128]{2,1,0:T(8,128)S(1)} %shard_map.47) | non-fusion elementwise | flops 139264 | bytes 835584 | tf_op jit(solution)/shard_map/convert_element_type | solution.py:193
  27.1 0.0 copy-start.1
  27.1 5.4 %all-to-all-start.1 = ((f16[8,136,128]{2,1,0:T(8,128)(2,1)}), f16[8,136,128]{2,1,0:T(8,128)(2,1)S(1)}, u32[]{:S(2)}, u32[]{:S(2)}) async-start(f16[8,136,128]{2,1,0:T(8,128)(2,1)} %convert_element_type.7), calls=%async_computation.1 | async-start | bytes 557056 | tf_op jit(solution)/shard_map/all_to_all | solution.py:192
  32.5 0.0 copy-done.1
  32.5 0.0 collective-permute-start.5
  32.6 1.2 %collective-permute-done.5 = bf16[128,256]{1,0:T(8,128)(2,1)S(1)} collective-permute-done((bf16[128,256]{1,0:T(8,128)(2,1)S(1)}, bf16[128,256]{1,0:T(8,128)(2,1)S(1)}, u32[]{:S(2)}, u32[]{:S(2)}) %collective-permute-start.5) | collective-permute-done | bytes 65568 | tf_op jit(solution)/shard_map/ppermute | solution.py:209
  33.8 5.4 %all-to-all-done.1 = f16[8,136,128]{2,1,0:T(8,128)(2,1)S(1)} async-done(((f16[8,136,128]{2,1,0:T(8,128)(2,1)}), f16[8,136,128]{2,1,0:T(8,128)(2,1)S(1)}, u32[]{:S(2)}, u32[]{:S(2)}) %all-to-all-start.1) | async-done | bytes 278560 | tf_op jit(solution)/shard_map/all_to_all | solution.py:192
  39.2 0.2 fusion.11
  39.4 0.1 fusion
  39.5 0.8 %fusion.1 = f32[64,256]{1,0:T(8,128)} fusion(bf16[256,256]{1,0:T(8,128)(2,1)S(1)} %bitcast.20, bf16[64,256]{1,0:T(8,128)(2,1)S(1)} %get-tuple-element.12, bf16[64,256]{1,0:T(8,128)(2,1)S(1)} %get-tuple-element.11), kind=kOutput, calls=%fused_computation.2 | convolution fusion | flops 17432576 | bytes 262144 | tf_op jit(solution)/shard_map/dot_general | solution.py:215
  (8 shorter events, 0.1 us)
Async XLA Ops:
  0.0 21.2 %collective-permute-start = (bf16[16,64,256]{2,1,0:T(8,128)(2,1)}, bf16[16,64,256]{2,1,0:T(8,128)(2,1)S(1)}, u32[]{:S(2)}, u32[]{:S(2)}) collective-permute-start(bf16[16,64,256]{2,1,0:T(8,128)(2,1)} %bitcast.15), channel_id=1, source_target_pairs={{0,1},{1,0},{2,3},{3,2},{4,5},{5,4},{6,7},{7,6},{8,9},{9,8},{10,11... | collective-permute-start | bytes 1572872 | tf_op jit(solution)/shard_map/ppermute | solution.py:167
  5.0 4.9 %copy-start.2 = (s32[64]{0:T(128)S(1)}, s32[64]{0:T(128)}, u32[]{:S(2)}) copy-start(s32[64]{0:T(128)} %param.7) | copy-start | bytes 772
  5.0 14.6 %copy-start = (bf16[64,16,256]{2,1,0:T(8,128)(2,1)S(1)}, bf16[64,16,256]{2,1,0:T(8,128)(2,1)}, u32[]{:S(2)}) copy-start(bf16[64,16,256]{2,1,0:T(8,128)(2,1)} %param.5) | copy-start | bytes 1572868
  5.0 19.9 %all-to-all-start = ((bf16[32,64,128]{2,1,0:T(8,128)(2,1)}), bf16[32,64,128]{2,1,0:T(8,128)(2,1)S(1)}, u32[]{:S(2)}, u32[]{:S(2)}) async-start(bf16[32,64,128]{2,1,0:T(8,128)(2,1)} %shard_map.46), calls=%async_computation | async-start | bytes 1048576 | tf_op jit(solution)/shard_map/all_to_all | solution.py:180
  9.9 9.6 %collective-permute-start.1 = (s32[64]{0:T(128)S(1)}, s32[64]{0:T(128)S(1)}, u32[]{:S(2)}, u32[]{:S(2)}) collective-permute-start(s32[64]{0:T(128)S(1)} %copy-done.2), channel_id=1, source_target_pairs={{0,1},{1,0},{2,3},{3,2},{4,5},{5,4},{6,7},{7,6},{8,9},{9,8},{10,11... | collective-permute-start | bytes 776 | tf_op jit(solution)/shard_map/ppermute | solution.py:167
  19.5 1.2 %collective-permute-start.2 = (s32[2,64]{1,0:T(2,128)S(1)}, s32[2,64]{1,0:T(2,128)S(1)}, u32[]{:S(2)}, u32[]{:S(2)}) collective-permute-start(s32[2,64]{1,0:T(2,128)S(1)} %get-tuple-element.16), channel_id=1, source_target_pairs={{0,2},{2,0},{4,6},{6,4},{8,10},{10,8},{12,14},{14,12},{16,18},{18,... | collective-permute-start | bytes 1544 | tf_op jit(solution)/shard_map/ppermute | solution.py:172
  19.6 2.0 %collective-permute-start.3 = (bf16[16,64,256]{2,1,0:T(8,128)(2,1)S(1)}, bf16[16,64,256]{2,1,0:T(8,128)(2,1)S(1)}, u32[]{:S(2)}, u32[]{:S(2)}) collective-permute-start(bf16[16,64,256]{2,1,0:T(8,128)(2,1)S(1)} %bitcast.16), channel_id=1, source_target_pairs={{0,2},{2,0},{4,6},{6,4},{8,10},{10,8},{12,14},{14,12},{16,18},{18,... | collective-permute-start | bytes 1572872 | tf_op jit(solution)/shard_map/ppermute | solution.py:175
  21.2 3.7 %collective-permute-start.4 = (bf16[16,64,256]{2,1,0:T(8,128)(2,1)S(1)}, bf16[16,64,256]{2,1,0:T(8,128)(2,1)S(1)}, u32[]{:S(2)}, u32[]{:S(2)}) collective-permute-start(bf16[16,64,256]{2,1,0:T(8,128)(2,1)S(1)} %collective-permute-done.refs_1_), channel_id=1, source_target_pairs={{0,2},{2,0},{4,6},{6,4},{8,10},{10,8},{12,14},{14,12},{16,18},{18,... | collective-permute-start | bytes 1572872 | tf_op jit(solution)/shard_map/ppermute | solution.py:177
  27.1 5.4 %copy-start.1 = (bf16[128,256]{1,0:T(8,128)(2,1)S(1)}, bf16[128,256]{1,0:T(8,128)(2,1)}, u32[]{:S(2)}) copy-start(bf16[128,256]{1,0:T(8,128)(2,1)} %param.4) | copy-start | bytes 196612
  27.1 12.1 %all-to-all-start.1 = ((f16[8,136,128]{2,1,0:T(8,128)(2,1)}), f16[8,136,128]{2,1,0:T(8,128)(2,1)S(1)}, u32[]{:S(2)}, u32[]{:S(2)}) async-start(f16[8,136,128]{2,1,0:T(8,128)(2,1)} %convert_element_type.7), calls=%async_computation.1 | async-start | bytes 557056 | tf_op jit(solution)/shard_map/all_to_all | solution.py:192
  32.5 1.3 %collective-permute-start.5 = (bf16[128,256]{1,0:T(8,128)(2,1)S(1)}, bf16[128,256]{1,0:T(8,128)(2,1)S(1)}, u32[]{:S(2)}, u32[]{:S(2)}) collective-permute-start(bf16[128,256]{1,0:T(8,128)(2,1)S(1)} %copy-done.1), channel_id=1, source_target_pairs={{0,2},{2,0},{4,6},{6,4},{8,10},{10,8},{12,14},{14,12},{16,18},{18,... | collective-permute-start | bytes 196616 | tf_op jit(solution)/shard_map/ppermute | solution.py:209

commit v4 on v3

--- a/solution.py
+++ b/solution.py
@@ -15,7 +15,7 @@
 
 def ring_of(count):
     stride = 3 if count % 3 else 1
-    return [-stride * n % count for n in range(count)]
+    return [(count // 2 - stride * n) % count for n in range(count)]
 
 
 def slab_kernel(p_hbm, o_hbm, p_ref, o_ref, in_sems, out_sems):
@@ -108,7 +108,7 @@
     parts = total_ref.shape[1] // lanes
     dests = out_ref.shape[0]
     for n in range(dests):
-        place = (n + dests // 2) % dests
+        place = ring_of(dests).index(n)
         for k in range(parts):
             out_ref[place, k * out_rows : (k + 1) * out_rows] = (
                 total_ref[n * out_rows : (n + 1) * out_rows, k * lanes : (k + 1) * lanes] * scale
@@ -138,7 +138,7 @@
         total = total.reshape(dests, out_rows, parts, part_width) * jnp.exp2(TOP - exponent)
         total = jnp.swapaxes(total, 1, 2).reshape(dests, parts * out_rows, part_width)
         note = jnp.full((dests, NOTE_ROWS, part_width), exponent)
-        return jnp.roll(jnp.concatenate([total, note], axis=1), dests // 2, axis=0)
+        return jnp.take(jnp.concatenate([total, note], axis=1), np.array(ring_of(dests)), axis=0)
     in_vmem = pl.BlockSpec(memory_space=pltpu.VMEM)
     return pl.pallas_call(
         functools.partial(fold_kernel, sector_count, out_rows),
@@ -187,8 +187,7 @@
     )
 
     partial = fold_tiles(arrived, edge_turns + others, lanes, my_blk, sector_count, out_rows)
-    middle = [(n - columns // 2) % columns for n in range(columns)]
-    groups = [[2 * n + c for n in middle] for c in range(2)]
+    groups = [[2 * n + c for n in ring_of(columns)] for c in range(2)]
     received = lax.all_to_all(
         partial.astype(jnp.float16),
         "sec",
@@ -197,7 +196,7 @@
         tiled=True,
         axis_index_groups=groups,
     ).astype(jnp.float32)
-    scales = jnp.exp2(received[:, -1:, :1] - TOP)
+    scales = jnp.exp2(received[:, -1:] - TOP)
     rows = jnp.sum(received[:, :-NOTE_ROWS] * scales, axis=0)
     rows = jnp.concatenate(jnp.split(rows, rows.shape[0] // out_rows), axis=1)
 

time: 40.7 us -> 40.3 us (level)
  no operation moved by 1% of the time
where the time goes in v4:
time: 40.3 us; the launch traced here: 40 us
  waiting for transfers between devices  18.2 us (45%)
  starting transfers between devices  15.9 us (39%)
  Pallas kernels  3.44 us (9%)
  other arithmetic  0.87 us (2%)
  matrix products  0.8 us (2%)
  local copies, waits for them, and re-layouts  0.52 us (1%)
    ppermute x2, waiting for transfers between devices, turn(): lax.ppermute(array, 'blk', [(j, (j + by) % blk_count) for j in range(blk_...  7.73 us
    all_to_all x1, starting transfers between devices, local(): lax.all_to_all(partial.astype(jnp.float16), 'sec', split_axis=0, concat_a...  5.42 us
    all_to_all x1, waiting for transfers between devices, local(): lax.all_to_all(partial.astype(jnp.float16), 'sec', split_axis=0, concat_a...  5.21 us
    all_to_all x1, starting transfers between devices, local(): lax.all_to_all(slabs, ('sec', 'blk'), split_axis=0, concat_axis=0, tiled=...  4.9 us
    ppermute x2, starting transfers between devices, turn(): lax.ppermute(array, 'blk', [(j, (j + by) % blk_count) for j in range(blk_...  4.8 us
    all_to_all x1, waiting for transfers between devices, local(): lax.all_to_all(slabs, ('sec', 'blk'), split_axis=0, concat_axis=0, tiled=...  3.31 us
    pallas_call x1, Pallas kernels, make_slabs(): pl.pallas_call(slab_kernel, out_shape=jax.ShapeDtypeStruct(shape, p3.dtyp...  1.99 us
    pallas_call x1, Pallas kernels, fold_tiles(): pl.pallas_call(functools.partial(fold_kernel, sector_count, out_rows), ou...  1.44 us
  transfers between devices with their start and end apart: 8, of which 6 were waited for; matrix products, arithmetic and copies ran while one was open for 1% of the time, Pallas kernels for 5%

profile of v4, /device:TPU:0, one launch (start us, length us, event | category | flops | bytes accessed | tf_op | source)
XLA Modules:
  0.0 40.0 jit_solution(2880543252111918607)
XLA Ops:
  0.0 3.0 %collective-permute-start = (bf16[16,64,256]{2,1,0:T(8,128)(2,1)}, bf16[16,64,256]{2,1,0:T(8,128)(2,1)S(1)}, u32[]{:S(2)}, u32[]{:S(2)}) collective-permute-start(bf16[16,64,256]{2,1,0:T(8,128)(2,1)} %bitcast.16), channel_id=1, source_target_pairs={{0,1},{1,0},{2,3},{3,2},{4,5},{5,4},{6,7},{7,6},{8,9},{9,8},{10,11... | collective-permute-start | bytes 1572872 | tf_op jit(solution)/shard_map/ppermute | solution.py:167
  3.0 2.0 %shard_map.46 = bf16[32,64,128]{2,1,0:T(8,128)(2,1)} custom-call(bf16[8,128,256]{2,1,0:T(8,128)(2,1)} %bitcast.19), custom_call_target="tpu_custom_call" | custom-call | tf_op jit(solution)/shard_map/pallas_call | solution.py:59
  5.0 0.0 copy-start.2
  5.0 0.0 copy-start
  5.0 4.9 %all-to-all-start = ((bf16[32,64,128]{2,1,0:T(8,128)(2,1)}), bf16[32,64,128]{2,1,0:T(8,128)(2,1)S(1)}, u32[]{:S(2)}, u32[]{:S(2)}) async-start(bf16[32,64,128]{2,1,0:T(8,128)(2,1)} %shard_map.46), calls=%async_computation | async-start | bytes 1048576 | tf_op jit(solution)/shard_map/all_to_all | solution.py:180
  9.9 0.0 copy-done.2
  9.9 1.8 %collective-permute-start.1 = (s32[64]{0:T(128)S(1)}, s32[64]{0:T(128)S(1)}, u32[]{:S(2)}, u32[]{:S(2)}) collective-permute-start(s32[64]{0:T(128)S(1)} %copy-done.2), channel_id=1, source_target_pairs={{0,1},{1,0},{2,3},{3,2},{4,5},{5,4},{6,7},{7,6},{8,9},{9,8},{10,11... | collective-permute-start | bytes 776 | tf_op jit(solution)/shard_map/ppermute | solution.py:167
  11.7 7.7 %collective-permute-done.1 = s32[64]{0:T(128)S(1)} collective-permute-done((s32[64]{0:T(128)S(1)}, s32[64]{0:T(128)S(1)}, u32[]{:S(2)}, u32[]{:S(2)}) %collective-permute-start.1) | collective-permute-done | bytes 288 | tf_op jit(solution)/shard_map/ppermute | solution.py:167
  19.5 0.1 collective-permute-start.2
  19.6 0.0 copy-done
  19.6 0.5 %collective-permute-start.3 = (bf16[16,64,256]{2,1,0:T(8,128)(2,1)S(1)}, bf16[16,64,256]{2,1,0:T(8,128)(2,1)S(1)}, u32[]{:S(2)}, u32[]{:S(2)}) collective-permute-start(bf16[16,64,256]{2,1,0:T(8,128)(2,1)S(1)} %bitcast.17), channel_id=1, source_target_pairs={{0,2},{2,0},{4,6},{6,4},{8,10},{10,8},{12,14},{14,12},{16,18},{18,... | collective-permute-start | bytes 1572872 | tf_op jit(solution)/shard_map/ppermute | solution.py:175
  20.1 0.6 %collective-permute-done.2 = s32[2,64]{1,0:T(2,128)S(1)} collective-permute-done((s32[2,64]{1,0:T(2,128)S(1)}, s32[2,64]{1,0:T(2,128)S(1)}, u32[]{:S(2)}, u32[]{:S(2)}) %collective-permute-start.2) | collective-permute-done | bytes 544 | tf_op jit(solution)/shard_map/ppermute | solution.py:172
  20.7 0.1 reshape.26
  20.8 0.1 copy.5
  20.9 0.1 copy.6
  20.9 0.1 broadcast_in_dim.15
  21.1 0.1 broadcast_in_dim.16.lane_ref
  21.2 0.0 collective-permute-done.refs_1_
  21.2 0.3 collective-permute-start.4
  21.4 0.1 collective-permute-done.3.refs_2_
  21.6 3.3 %all-to-all-done.slab_ref = bf16[32,64,128]{2,1,0:T(8,128)(2,1)S(1)} async-done(((bf16[32,64,128]{2,1,0:T(8,128)(2,1)}), bf16[32,64,128]{2,1,0:T(8,128)(2,1)S(1)}, u32[]{:S(2)}, u32[]{:S(2)}) %all-to-all-start) | async-done | bytes 524320 | tf_op jit(solution)/shard_map/all_to_all | solution.py:180
  24.9 0.0 collective-permute-done.4.refs_3_
  24.9 1.4 %shard_map.47 = f32[8,136,128]{2,1,0:T(8,128)S(1)} custom-call(s32[1]{0:T(128)} %bitcast.blk_ref, s32[16,1,256]{2,1,0:T(1,128)S(1)} %broadcast_in_dim.16.lane_ref, bf16[32,64,128]{2,1,0:T(8,128)(2,1)S(1)} %all-to-all-done.slab_ref, bf16[16,64,256]{2,1,0:T(8,128)(2,1)S(1)} %bitcast.18, bf16[16,64,256]{2,1,0:T(8,128)(2,1)S(1)} %collective-permute-done.refs_1_, ...), custom_call_target="tpu_custom_call" | custom-call | tf_op jit(solution)/shard_map/pallas_call | solution.py:143
  26.4 0.8 %convert_element_type.7 = f16[8,136,128]{2,1,0:T(8,128)(2,1)} convert(f32[8,136,128]{2,1,0:T(8,128)S(1)} %shard_map.47) | non-fusion elementwise | flops 139264 | bytes 835584 | tf_op jit(solution)/shard_map/convert_element_type | solution.py:192
  27.1 0.0 copy-start.1
  27.1 5.4 %all-to-all-start.1 = ((f16[8,136,128]{2,1,0:T(8,128)(2,1)}), f16[8,136,128]{2,1,0:T(8,128)(2,1)S(1)}, u32[]{:S(2)}, u32[]{:S(2)}) async-start(f16[8,136,128]{2,1,0:T(8,128)(2,1)} %convert_element_type.7), calls=%async_computation.1 | async-start | bytes 557056 | tf_op jit(solution)/shard_map/all_to_all | solution.py:191
  32.5 0.0 copy-done.1
  32.5 0.0 collective-permute-start.5
  32.6 1.2 %collective-permute-done.5 = bf16[128,256]{1,0:T(8,128)(2,1)S(1)} collective-permute-done((bf16[128,256]{1,0:T(8,128)(2,1)S(1)}, bf16[128,256]{1,0:T(8,128)(2,1)S(1)}, u32[]{:S(2)}, u32[]{:S(2)}) %collective-permute-start.5) | collective-permute-done | bytes 65568 | tf_op jit(solution)/shard_map/ppermute | solution.py:208
  33.8 5.2 %all-to-all-done.1 = f16[8,136,128]{2,1,0:T(8,128)(2,1)S(1)} async-done(((f16[8,136,128]{2,1,0:T(8,128)(2,1)}), f16[8,136,128]{2,1,0:T(8,128)(2,1)S(1)}, u32[]{:S(2)}, u32[]{:S(2)}) %all-to-all-start.1) | async-done | bytes 278560 | tf_op jit(solution)/shard_map/all_to_all | solution.py:191
  39.2 0.8 %fusion.1 = f32[64,256]{1,0:T(8,128)} fusion(bf16[256,256]{1,0:T(8,128)(2,1)S(1)} %bitcast.21, bf16[64,256]{1,0:T(8,128)(2,1)S(1)} %get-tuple-element.12, bf16[64,256]{1,0:T(8,128)(2,1)S(1)} %get-tuple-element.11), kind=kOutput, calls=%fused_computation.2 | convolution fusion | flops 17432576 | bytes 262144 | tf_op jit(solution)/shard_map/dot_general | solution.py:214
  (10 shorter events, 0.2 us)
Async XLA Ops:
  0.0 21.2 %collective-permute-start = (bf16[16,64,256]{2,1,0:T(8,128)(2,1)}, bf16[16,64,256]{2,1,0:T(8,128)(2,1)S(1)}, u32[]{:S(2)}, u32[]{:S(2)}) collective-permute-start(bf16[16,64,256]{2,1,0:T(8,128)(2,1)} %bitcast.16), channel_id=1, source_target_pairs={{0,1},{1,0},{2,3},{3,2},{4,5},{5,4},{6,7},{7,6},{8,9},{9,8},{10,11... | collective-permute-start | bytes 1572872 | tf_op jit(solution)/shard_map/ppermute | solution.py:167
  5.0 4.9 %copy-start.2 = (s32[64]{0:T(128)S(1)}, s32[64]{0:T(128)}, u32[]{:S(2)}) copy-start(s32[64]{0:T(128)} %param.7) | copy-start | bytes 772
  5.0 14.6 %copy-start = (bf16[64,16,256]{2,1,0:T(8,128)(2,1)S(1)}, bf16[64,16,256]{2,1,0:T(8,128)(2,1)}, u32[]{:S(2)}) copy-start(bf16[64,16,256]{2,1,0:T(8,128)(2,1)} %param.5) | copy-start | bytes 1572868
  5.0 19.9 %all-to-all-start = ((bf16[32,64,128]{2,1,0:T(8,128)(2,1)}), bf16[32,64,128]{2,1,0:T(8,128)(2,1)S(1)}, u32[]{:S(2)}, u32[]{:S(2)}) async-start(bf16[32,64,128]{2,1,0:T(8,128)(2,1)} %shard_map.46), calls=%async_computation | async-start | bytes 1048576 | tf_op jit(solution)/shard_map/all_to_all | solution.py:180
  9.9 9.6 %collective-permute-start.1 = (s32[64]{0:T(128)S(1)}, s32[64]{0:T(128)S(1)}, u32[]{:S(2)}, u32[]{:S(2)}) collective-permute-start(s32[64]{0:T(128)S(1)} %copy-done.2), channel_id=1, source_target_pairs={{0,1},{1,0},{2,3},{3,2},{4,5},{5,4},{6,7},{7,6},{8,9},{9,8},{10,11... | collective-permute-start | bytes 776 | tf_op jit(solution)/shard_map/ppermute | solution.py:167
  19.5 1.2 %collective-permute-start.2 = (s32[2,64]{1,0:T(2,128)S(1)}, s32[2,64]{1,0:T(2,128)S(1)}, u32[]{:S(2)}, u32[]{:S(2)}) collective-permute-start(s32[2,64]{1,0:T(2,128)S(1)} %get-tuple-element.16), channel_id=1, source_target_pairs={{0,2},{2,0},{4,6},{6,4},{8,10},{10,8},{12,14},{14,12},{16,18},{18,... | collective-permute-start | bytes 1544 | tf_op jit(solution)/shard_map/ppermute | solution.py:172
  19.6 2.0 %collective-permute-start.3 = (bf16[16,64,256]{2,1,0:T(8,128)(2,1)S(1)}, bf16[16,64,256]{2,1,0:T(8,128)(2,1)S(1)}, u32[]{:S(2)}, u32[]{:S(2)}) collective-permute-start(bf16[16,64,256]{2,1,0:T(8,128)(2,1)S(1)} %bitcast.17), channel_id=1, source_target_pairs={{0,2},{2,0},{4,6},{6,4},{8,10},{10,8},{12,14},{14,12},{16,18},{18,... | collective-permute-start | bytes 1572872 | tf_op jit(solution)/shard_map/ppermute | solution.py:175
  21.2 3.7 %collective-permute-start.4 = (bf16[16,64,256]{2,1,0:T(8,128)(2,1)S(1)}, bf16[16,64,256]{2,1,0:T(8,128)(2,1)S(1)}, u32[]{:S(2)}, u32[]{:S(2)}) collective-permute-start(bf16[16,64,256]{2,1,0:T(8,128)(2,1)S(1)} %collective-permute-done.refs_1_), channel_id=1, source_target_pairs={{0,2},{2,0},{4,6},{6,4},{8,10},{10,8},{12,14},{14,12},{16,18},{18,... | collective-permute-start | bytes 1572872 | tf_op jit(solution)/shard_map/ppermute | solution.py:177
  27.1 5.4 %copy-start.1 = (bf16[128,256]{1,0:T(8,128)(2,1)S(1)}, bf16[128,256]{1,0:T(8,128)(2,1)}, u32[]{:S(2)}) copy-start(bf16[128,256]{1,0:T(8,128)(2,1)} %param.4) | copy-start | bytes 196612
  27.1 11.9 %all-to-all-start.1 = ((f16[8,136,128]{2,1,0:T(8,128)(2,1)}), f16[8,136,128]{2,1,0:T(8,128)(2,1)S(1)}, u32[]{:S(2)}, u32[]{:S(2)}) async-start(f16[8,136,128]{2,1,0:T(8,128)(2,1)} %convert_element_type.7), calls=%async_computation.1 | async-start | bytes 557056 | tf_op jit(solution)/shard_map/all_to_all | solution.py:191
  32.5 1.3 %collective-permute-start.5 = (bf16[128,256]{1,0:T(8,128)(2,1)S(1)}, bf16[128,256]{1,0:T(8,128)(2,1)S(1)}, u32[]{:S(2)}, u32[]{:S(2)}) collective-permute-start(bf16[128,256]{1,0:T(8,128)(2,1)S(1)} %copy-done.1), channel_id=1, source_target_pairs={{0,2},{2,0},{4,6},{6,4},{8,10},{10,8},{12,14},{14,12},{16,18},{18,... | collective-permute-start | bytes 196616 | tf_op jit(solution)/shard_map/ppermute | solution.py:208
